TPU v7x, 32 devices: a whole 2x2x4 slice. The times are simulated.
32 devices in a mesh: batch: 8 (over y, x, core), tensor: 4 (over z).
Axes of the slice: x: 2, y: 2, z: 4, core: 2. Of those that a mesh axis runs over, the one named last changes fastest.
Arguments:
- tokens: bfloat16 [8192, 1024], P('batch'), may hold values from -6 to 6
- segment_ids: int32 [8, 1024], P('batch'), may hold values from 0 to 3, never falling along the last dimension, each value on 1 to 512 neighbouring positions
- attention_gain: float32 [1024], replicated, may hold values from 0.5 to 1.5
- attention_shift: float32 [1024], replicated, may hold values from -1.25 to 1.25
- joint_weight: bfloat16 [3, 1024, 1024], P(None, None, 'tensor'), may hold values from -0.1875 to 0.1875
- joint_bias: float32 [3, 1024], P(None, 'tensor'), may hold values from -1.75 to 1.75
- output_weight: bfloat16 [1024, 1024], P('tensor'), may hold values from -0.75 to 0.75
- output_bias: float32 [1024], replicated, may hold values from -1.75 to 1.75
- mixer_gain: float32 [1024], replicated, may hold values from 0.5 to 1.5
- mixer_shift: float32 [1024], replicated, may hold values from -1.25 to 1.25
- up_weight: bfloat16 [1024, 4096], P(None, 'tensor'), may hold values from -0.1875 to 0.1875
- up_bias: float32 [4096], P('tensor'), may hold values from -1.75 to 1.75
- down_weight: bfloat16 [4096, 1024], P('tensor'), may hold values from -0.125 to 0.125
- down_bias: float32 [1024], replicated, may hold values from -1.75 to 1.75
- prefix_table: float32 [10, 1024], replicated, may hold values from -6 to 6
- inner_weight: bfloat16 [1024, 512], replicated, may hold values from -0.1875 to 0.1875
- inner_bias: float32 [512], replicated, may hold values from -1.75 to 1.75
- outer_weight: bfloat16 [512, 2, 1024], P(None, None, 'tensor'), may hold values from -0.5 to 0.5
- outer_bias: float32 [2, 1024], P(None, 'tensor'), may hold values from -1.75 to 1.75
- cotangent: bfloat16 [8192, 1024], P('batch'), may hold values from -6 to 6
Outputs:
- block_output: bfloat16 [8192, 1024], P('batch', 'tensor')
- tokens_gradient: bfloat16 [8192, 1024], P('batch', 'tensor')
- attention_gain_gradient: float32 [1024], P('tensor')
- attention_shift_gradient: float32 [1024], P('tensor')
- joint_weight_gradient: float32 [3, 1024, 1024], P(None, 'batch', 'tensor')
- joint_bias_gradient: float32 [3, 1024], P(None, 'tensor')
- output_weight_gradient: float32 [1024, 1024], P('tensor', 'batch')
- output_bias_gradient: float32 [1024], P('tensor')
- mixer_gain_gradient: float32 [1024], P('tensor')
- mixer_shift_gradient: float32 [1024], P('tensor')
- up_weight_gradient: float32 [1024, 4096], P('batch', 'tensor')
- up_bias_gradient: float32 [4096], P('tensor')
- down_weight_gradient: float32 [4096, 1024], P('tensor', 'batch')
- down_bias_gradient: float32 [1024], P('tensor')
- prefix_table_gradient: float32 [10, 1024], replicated
- inner_weight_gradient: float32 [1024, 512], replicated
- inner_bias_gradient: float32 [512], replicated
- outer_weight_gradient: float32 [512, 2, 1024], P('batch', None, 'tensor')
- outer_bias_gradient: float32 [2, 1024], P(None, 'tensor')
Inputs may be any that keep to these rules, and one draw needn't show every extreme that they name: `segment_ids`: along each packed row the ids never fall, and no segment holds more than half of 1024 tokens.
All inputs are finite; a program needn't handle non-finite values.
Results may differ from a plain program's by a relative error of at most 0.013.
Values sent between devices are 32-bit elements; how exact they have to be, the bound alone decides.
No kernel may reach another device: no remote copies, remote signals or barrier semaphores. Data moves between devices by JAX's collectives and lax.ppermute only.
A program may use at most 192 MiB of HBM per device.

v0:
```python
import jax
import jax.numpy as jnp
from jax import lax
from jax.sharding import PartitionSpec as P

HD = 64


EPSILON = 1e-05
PRECISE = lax.Precision.HIGHEST
NEGATIVE = -1e30


def normalize(values):
    centered = values - jnp.mean(values, axis=-1, keepdims=True)
    inverse = lax.rsqrt(jnp.mean(centered * centered, axis=-1, keepdims=True) + EPSILON)
    return (centered * inverse, inverse)


def activate(values):
    return jax.nn.gelu(values, approximate=True)


def to_heads(flat_rows, row_count):
    tokens_all, width_all = flat_rows.shape
    return flat_rows.reshape(row_count, tokens_all // row_count, width_all // HD, HD).transpose(
        0, 2, 1, 3
    )


def from_heads(per_head):
    row_count, head_count, length, head_size = per_head.shape
    return per_head.transpose(0, 2, 1, 3).reshape(row_count * length, head_count * head_size)


def score_blocks(queries, key_heads, prefix_keys, row_segments):
    length = row_segments.shape[0]
    position = lax.broadcasted_iota(jnp.int32, (length, length), 0)
    earlier = lax.broadcasted_iota(jnp.int32, (length, length), 1) <= position
    allowed = (row_segments[:, None] == row_segments[None, :]) & earlier
    token_scores = jnp.einsum(
        "hqd,hkd->hqk", queries, key_heads, preferred_element_type=jnp.float32
    )
    token_scores = jnp.where(allowed[None], token_scores, NEGATIVE)
    prefix_scores = jnp.einsum(
        "hpd,hqd->hpq", prefix_keys, queries, preferred_element_type=jnp.float32
    )
    return (token_scores, prefix_scores)


def attend(queries, key_heads, value_heads, row_segments, prefix_keys, prefix_values):
    token_scores, prefix_scores = score_blocks(queries, key_heads, prefix_keys, row_segments)
    row_max = jnp.maximum(jnp.max(token_scores, axis=-1), jnp.max(prefix_scores, axis=1))
    token_expo = jnp.exp(token_scores - row_max[..., None])
    prefix_expo = jnp.exp(prefix_scores - row_max[:, None, :])
    row_total = jnp.sum(token_expo, axis=-1) + jnp.sum(prefix_expo, axis=1)
    log_total = row_max + jnp.log(row_total)
    token_low = (token_expo / row_total[..., None]).astype(jnp.bfloat16)
    prefix_low = (prefix_expo / row_total[:, None, :]).astype(jnp.bfloat16)
    attended = jnp.einsum(
        "hqk,hkd->hqd", token_low, value_heads, preferred_element_type=jnp.float32
    )
    attended = attended + jnp.einsum(
        "hpq,hpd->hqd", prefix_low, prefix_values, preferred_element_type=jnp.float32
    )
    return (attended, log_total)


def attend_back(
    queries, key_heads, value_heads, row_segments, grad_heads, log_total, prefix_keys, prefix_values
):
    token_scores, prefix_scores = score_blocks(queries, key_heads, prefix_keys, row_segments)
    token_probs = jnp.exp(token_scores - log_total[..., None])
    prefix_probs = jnp.exp(prefix_scores - log_total[:, None, :])
    token_low = token_probs.astype(jnp.bfloat16)
    prefix_low = prefix_probs.astype(jnp.bfloat16)
    grad_values = jnp.einsum(
        "hqk,hqd->hkd", token_low, grad_heads, preferred_element_type=jnp.float32
    )
    grad_prefix_values = jnp.einsum(
        "hpq,hqd->hpd", prefix_low, grad_heads, preferred_element_type=jnp.float32
    )
    grad_token_probs = jnp.einsum(
        "hqd,hkd->hqk", grad_heads, value_heads, preferred_element_type=jnp.float32
    )
    grad_prefix_probs = jnp.einsum(
        "hqd,hpd->hpq", grad_heads, prefix_values, preferred_element_type=jnp.float32
    )
    delta_rows = jnp.sum(token_probs * grad_token_probs, axis=-1) + jnp.sum(
        prefix_probs * grad_prefix_probs, axis=1
    )
    grad_token_scores = (token_probs * (grad_token_probs - delta_rows[..., None])).astype(
        jnp.bfloat16
    )
    grad_prefix_scores = (prefix_probs * (grad_prefix_probs - delta_rows[:, None, :])).astype(
        jnp.bfloat16
    )
    grad_queries = jnp.einsum(
        "hqk,hkd->hqd", grad_token_scores, key_heads, preferred_element_type=jnp.float32
    )
    grad_queries = grad_queries + jnp.einsum(
        "hpq,hpd->hqd", grad_prefix_scores, prefix_keys, preferred_element_type=jnp.float32
    )
    grad_keys = jnp.einsum(
        "hqk,hqd->hkd", grad_token_scores, queries, preferred_element_type=jnp.float32
    )
    grad_prefix_keys = jnp.einsum(
        "hpq,hqd->hpd", grad_prefix_scores, queries, preferred_element_type=jnp.float32
    )
    return (grad_queries, grad_keys, grad_values, grad_prefix_keys, grad_prefix_values)


def shards(
    tokens,
    segment_ids,
    attention_gain,
    attention_shift,
    joint_weight,
    joint_bias,
    output_weight,
    output_bias,
    mixer_gain,
    mixer_shift,
    up_weight,
    up_bias,
    down_weight,
    down_bias,
    prefix_table,
    inner_weight,
    inner_bias,
    outer_weight,
    outer_bias,
    cotangent,
):
    row_count = segment_ids.shape[0]
    local_width = joint_weight.shape[2]
    prefix_count = prefix_table.shape[0]
    query_scale = HD ** (-0.5)
    column_start = lax.axis_index("tensor") * local_width

    def own_columns(values):
        return lax.dynamic_slice_in_dim(values, column_start, local_width, values.ndim - 1)

    tokens_float = tokens.astype(jnp.float32)
    normed_in, inverse_in = normalize(tokens_float)
    attention_in = (normed_in * attention_gain + attention_shift).astype(jnp.bfloat16)
    joint_proj = (
        jnp.einsum("td,kde->tke", attention_in, joint_weight, preferred_element_type=jnp.float32)
        + joint_bias[None]
    )
    queries = to_heads((joint_proj[:, 0] * query_scale).astype(jnp.bfloat16), row_count)
    key_heads = to_heads(joint_proj[:, 1].astype(jnp.bfloat16), row_count)
    value_heads = to_heads(joint_proj[:, 2].astype(jnp.bfloat16), row_count)
    hidden_prefix = jnp.tanh(
        jnp.dot(prefix_table, inner_weight.astype(jnp.float32), precision=PRECISE) + inner_bias
    )
    outer_float = outer_weight.astype(jnp.float32)
    prefix_pairs = (
        jnp.einsum("pr,rke->pke", hidden_prefix, outer_float, precision=PRECISE) + outer_bias[None]
    )
    prefix_keys = (
        prefix_pairs[:, 0].reshape(prefix_count, -1, HD).transpose(1, 0, 2).astype(jnp.bfloat16)
    )
    prefix_values = (
        prefix_pairs[:, 1].reshape(prefix_count, -1, HD).transpose(1, 0, 2).astype(jnp.bfloat16)
    )

    def forward_row(row_items):
        return attend(
            row_items[0], row_items[1], row_items[2], row_items[3], prefix_keys, prefix_values
        )

    attended_heads, log_total = lax.map(forward_row, (queries, key_heads, value_heads, segment_ids))
    attended = from_heads(attended_heads).astype(jnp.bfloat16)
    attention_out = lax.psum(
        jnp.dot(attended, output_weight, preferred_element_type=jnp.float32), "tensor"
    )
    residual = tokens_float + attention_out + output_bias
    normed_mid, inverse_mid = normalize(residual)
    mixer_in = (normed_mid * mixer_gain + mixer_shift).astype(jnp.bfloat16)
    pre_act = jnp.dot(mixer_in, up_weight, preferred_element_type=jnp.float32) + up_bias
    activated = activate(pre_act).astype(jnp.bfloat16)
    mixer_share = lax.psum_scatter(
        jnp.dot(activated, down_weight, preferred_element_type=jnp.float32),
        "tensor",
        scatter_dimension=1,
        tiled=True,
    )
    block_output = (own_columns(residual + down_bias) + mixer_share).astype(jnp.bfloat16)
    cotangent_float = cotangent.astype(jnp.float32)
    down_gradient = jnp.einsum(
        "tf,td->fd", activated, cotangent, preferred_element_type=jnp.float32
    )
    grad_act = jnp.einsum("td,fd->tf", cotangent, down_weight, preferred_element_type=jnp.float32)
    pullback = jax.vjp(activate, pre_act)[1]
    grad_pre = pullback(grad_act)[0].astype(jnp.bfloat16)
    up_gradient = jnp.einsum("td,tf->df", mixer_in, grad_pre, preferred_element_type=jnp.float32)
    up_bias_sum = jnp.sum(grad_pre.astype(jnp.float32), axis=0)
    grad_mixer = lax.psum(
        jnp.einsum("tf,df->td", grad_pre, up_weight, preferred_element_type=jnp.float32), "tensor"
    )
    mixer_gain_sum = jnp.sum(grad_mixer * normed_mid, axis=0)
    mixer_shift_sum = jnp.sum(grad_mixer, axis=0)
    scaled_mid = grad_mixer * mixer_gain
    grad_residual = cotangent_float + inverse_mid * (
        scaled_mid
        - jnp.mean(scaled_mid, axis=-1, keepdims=True)
        - normed_mid * jnp.mean(scaled_mid * normed_mid, axis=-1, keepdims=True)
    )
    output_bias_sum = jnp.sum(grad_residual, axis=0)
    grad_res_low = grad_residual.astype(jnp.bfloat16)
    output_gradient = jnp.einsum(
        "te,td->ed", attended, grad_res_low, preferred_element_type=jnp.float32
    )
    grad_attended = jnp.einsum(
        "td,ed->te", grad_res_low, output_weight, preferred_element_type=jnp.float32
    ).astype(jnp.bfloat16)
    grad_heads = to_heads(grad_attended, row_count)

    def backward_row(row_items):
        return attend_back(
            row_items[0],
            row_items[1],
            row_items[2],
            row_items[3],
            row_items[4],
            row_items[5],
            prefix_keys,
            prefix_values,
        )

    grad_queries, grad_keys, grad_values, grad_pkeys, grad_pvalues = lax.map(
        backward_row, (queries, key_heads, value_heads, segment_ids, grad_heads, log_total)
    )
    grad_joint = jnp.stack(
        [
            from_heads(grad_queries).astype(jnp.bfloat16) * query_scale,
            from_heads(grad_keys).astype(jnp.bfloat16),
            from_heads(grad_values).astype(jnp.bfloat16),
        ],
        axis=1,
    )
    joint_gradient = jnp.einsum(
        "td,tke->kde", attention_in, grad_joint, preferred_element_type=jnp.float32
    )
    joint_bias_sum = jnp.sum(grad_joint.astype(jnp.float32), axis=0)
    grad_attention_part = jnp.einsum(
        "tke,kde->td", grad_joint, joint_weight, preferred_element_type=jnp.float32
    )
    grad_attention = lax.psum(grad_attention_part, "tensor")
    scaled_in = grad_attention * attention_gain
    grad_full = grad_residual + inverse_in * (
        scaled_in
        - jnp.mean(scaled_in, axis=-1, keepdims=True)
        - normed_in * jnp.mean(scaled_in * normed_in, axis=-1, keepdims=True)
    )
    tokens_gradient = own_columns(grad_full).astype(jnp.bfloat16)
    attention_gain_sum = own_columns(jnp.sum(grad_attention * normed_in, axis=0))
    attention_shift_sum = own_columns(jnp.sum(grad_attention, axis=0))
    prefix_key_grad = (
        jnp.sum(grad_pkeys, axis=0).transpose(1, 0, 2).reshape(prefix_count, local_width)
    )
    prefix_value_grad = (
        jnp.sum(grad_pvalues, axis=0).transpose(1, 0, 2).reshape(prefix_count, local_width)
    )
    grad_prefix_part = jnp.stack([prefix_key_grad, prefix_value_grad], axis=1)
    grad_prefix = lax.psum(grad_prefix_part, "batch")
    outer_full = jnp.einsum("pr,pke->rke", hidden_prefix, grad_prefix, precision=PRECISE)
    outer_rows = outer_full.shape[0] // lax.axis_size("batch")
    outer_total = lax.dynamic_slice_in_dim(
        outer_full, lax.axis_index("batch") * outer_rows, outer_rows, 0
    )
    outer_bias_total = jnp.sum(grad_prefix, axis=0)
    grad_hidden_part = jnp.einsum("pke,rke->pr", grad_prefix, outer_float, precision=PRECISE)
    grad_hidden_prefix = lax.psum(grad_hidden_part, "tensor")
    grad_inner = grad_hidden_prefix * (1.0 - hidden_prefix * hidden_prefix)
    inner_total = jnp.einsum("pd,pr->dr", prefix_table, grad_inner, precision=PRECISE)
    inner_bias_total = jnp.sum(grad_inner, axis=0)
    table_total = jnp.einsum(
        "pr,dr->pd", grad_inner, inner_weight.astype(jnp.float32), precision=PRECISE
    )
    joint_total, output_total, up_total, down_total = (
        lax.psum_scatter(joint_gradient, "batch", scatter_dimension=1, tiled=True),
        lax.psum_scatter(output_gradient, "batch", scatter_dimension=1, tiled=True),
        lax.psum_scatter(up_gradient, "batch", scatter_dimension=0, tiled=True),
        lax.psum_scatter(down_gradient, "batch", scatter_dimension=1, tiled=True),
    )
    small_totals = lax.psum(
        (
            joint_bias_sum,
            up_bias_sum,
            attention_gain_sum,
            attention_shift_sum,
            own_columns(mixer_gain_sum),
            own_columns(mixer_shift_sum),
            own_columns(output_bias_sum),
            own_columns(jnp.sum(cotangent_float, axis=0)),
        ),
        "batch",
    )
    return (
        block_output,
        tokens_gradient,
        small_totals[2],
        small_totals[3],
        joint_total,
        small_totals[0],
        output_total,
        small_totals[6],
        small_totals[4],
        small_totals[5],
        up_total,
        small_totals[1],
        down_total,
        small_totals[7],
        table_total,
        inner_total,
        inner_bias_total,
        outer_total,
        outer_bias_total,
    )


def solution(mesh):
    placed = (
        P("batch", None),
        P("batch", None),
        P(),
        P(),
        P(None, None, "tensor"),
        P(None, "tensor"),
        P("tensor", None),
        P(),
        P(),
        P(),
        P(None, "tensor"),
        P("tensor"),
        P("tensor", None),
        P(),
        P(),
        P(),
        P(),
        P(None, None, "tensor"),
        P(None, "tensor"),
        P("batch", None),
    )
    return jax.shard_map(
        shards,
        mesh=mesh,
        in_specs=placed,
        out_specs=(
            P("batch", "tensor"),
            P("batch", "tensor"),
            P("tensor"),
            P("tensor"),
            P(None, "batch", "tensor"),
            P(None, "tensor"),
            P("tensor", "batch"),
            P("tensor"),
            P("tensor"),
            P("tensor"),
            P("batch", "tensor"),
            P("tensor"),
            P("tensor", "batch"),
            P("tensor"),
            P(),
            P(),
            P(),
            P("batch", None, "tensor"),
            P(None, "tensor"),
        ),
        check_vma=False,
    )
```

profile of v0, /device:TPU:0, one launch (start us, length us, event | category | flops | bytes accessed | tf_op | source)
XLA Modules:
  0.0 891.0 jit_solution(17162762863494344516)
XLA Ops:
  7.4 2.1 convert_reduce_fusion
  9.5 2.3 fusion.8
  13.8 4.2 fusion.78
  19.2 7.8 select_reduce_fusion
  27.1 8.8 fusion
  35.9 8.2 fusion.5
  45.2 2.7 fusion.80
  48.0 157.8 %all-reduce.5.cloned.1.call-done = f32[1024,1024]{1,0:T(8,128)} async-done(((f32[1024,1024]{1,0:T(8,128)}), f32[1024,1024]{1,0:T(8,128)}) %all-reduce.5.cloned.1.call-update) | async-done | bytes 4194320 | tf_op jit(solution)/shard_map/psum | solution.py:175
  205.8 3.5 fusion.74
  210.0 2.4 copy-done.50
  212.4 2.4 fusion.67
  214.9 5.9 convert_reduce_fusion.2
  222.2 4.3 fusion.81
  226.5 154.1 %all-reduce.7.cloned.1.call-done = f32[1024,1024]{1,0:T(8,128)} async-done(((f32[1024,1024]{1,0:T(8,128)}), f32[1024,1024]{1,0:T(8,128)}) %all-reduce.7.cloned.1.call-update) | async-done | bytes 4194320 | tf_op jit(solution)/shard_map/psum | solution.py:199
  380.6 5.2 multiply_reduce_fusion.1
  386.6 3.8 fusion.73
  390.4 1.9 copy-done.4
  394.8 10.5 %fusion.20 = bf16[4,1024,64]{1,2,0:T(8,128)(2,1)} fusion(bf16[4,1024,64]{1,2,0:T(8,128)(2,1)} %bitcast.123, f32[4,1024,1024]{1,2,0:T(8,128)} %get-tuple-element.164, f32[4,1024]{1,0:T(4,128)S(1)} %get-tuple-element.148, pred[1024,1024]{0,1:T(8,128)(4,1)S(1)} %fusion.17), kind=kOutput, calls=%fused_computation.53 | convolution fusion | flops 549715968 | bytes 18890752 | tf_op jit(solution)/shard_map/while/body/eval_jaxpr/hqk,hqd->hkd/dot_general | solution.py:77
  405.2 12.0 %multiply_reduce_fusion = (f32[4,1024]{1,0:T(4,128)S(1)}, f32[4,1024,1024]{1,2,0:T(8,128)}) fusion(f32[4,1024,1024]{1,2,0:T(8,128)} %get-tuple-element.164, f32[4,1024]{1,0:T(4,128)S(1)} %get-tuple-element.148, pred[1024,1024]{0,1:T(8,128)(4,1)S(1)} %fusion.17, bf16[4,1024,64]{1,2,0:T(8,128)(2,1)} %bitcast.124, bf16[4,1024,64]{1,2,0:T(8,128)(2,1)} %bitcast.131), kind=kOutput, calls=%fused_computation.1 | convolution fusion | flops 553644032 | bytes 35684352 | tf_op jit(solution)/shard_map/while/body/eval_jaxpr/hqd,hkd->hqk/dot_general | solution.py:83
  417.3 2.0 copy.65
  419.3 12.6 %multiply_convert_fusion = bf16[4,1024,1024]{1,2,0:T(8,128)(2,1)S(1)} fusion(f32[4,1024,1024]{1,2,0:T(8,128)} %get-tuple-element.168, f32[4,1024,1024]{1,2,0:T(8,128)} %get-tuple-element.164, f32[4,1024]{1,0:T(4,128)S(1)} %add.231, f32[4,1024]{1,0:T(4,128)S(1)} %get-tuple-element.148, pred[1024,1024]{0,1:T(8,128)(4,1)S(1)} %fusion.17), kind=kLoop, calls=%fused_computation | loop fusion | flops 20971520 | bytes 43024384 | tf_op jit(solution)/shard_map/while/body/eval_jaxpr/convert_element_type | solution.py:92
  432.1 2.7 convolution_convert_fusion
  437.2 5.8 fusion.24
  444.3 5.5 convolution_bitcast_fusion
  450.5 6.9 fusion.65
  457.5 5.9 convolution_bitcast_fusion.1
  463.5 4.0 fusion.33
  467.8 7.5 fusion.66
  476.0 7.9 fusion.64
  483.9 1.4 dynamic-slice.5
  485.3 1.3 dynamic_slice.67
  486.6 1.3 dynamic_slice.68
  491.3 1.6 convert_reduce_fusion.3
  493.0 111.0 %all-reduce.9.cloned.1.call-done = f32[1024,1024]{1,0:T(8,128)} async-done(((f32[1024,1024]{1,0:T(8,128)}), f32[1024,1024]{1,0:T(8,128)}) %all-reduce.9.cloned.1.call-update) | async-done | bytes 4194320 | tf_op jit(solution)/shard_map/psum | solution.py:250
  604.0 6.1 fusion.70
  610.2 26.6 %all-reduce = (f32[256]{0:T(256)}, f32[256]{0:T(256)}, f32[3,256]{1,0:T(4,128)}, f32[256]{0:T(256)}, f32[256]{0:T(256)}, /*index=5*/f32[256]{0:T(256)}, f32[1024]{0:T(1024)}, f32[256]{0:T(256)}, f32[10,2,256]{2,0,1:T(8,128)S(1)}) all-reduce(f32[256]{0:T(256)S(1)} %dynamic_slice.64, ...), channel_id=1, replica_groups=mesh['batch'=8,'tensor'=4] {'batch'}, use_global_device_ids=true, to_apply=%region_19.20 | all-reduce | flops 8448 | bytes 67584 | tf_op jit(solution)/shard_map/psum | solution.py:288
  639.8 18.5 %psum.103 = f32[10,512]{1,0:T(8,128)S(1)} all-reduce(f32[10,512]{1,0:T(8,128)S(1)} %convolution_bitcast_fusion.5), channel_id=1, replica_groups=mesh['batch'=8,'tensor'=4] {'tensor'}, use_global_device_ids=true, to_apply=%region_39.40 | all-reduce | flops 5120 | bytes 40960 | tf_op jit(solution)/shard_map/psum | solution.py:275
  658.3 3.2 convolution_bitcast_fusion.2
  661.5 3.0 copy.71
  665.1 3.2 fusion.27
  668.3 1.6 fusion.63
  669.9 13.3 %reduce-scatter.6.cloned.1.call-done = f32[1024,256]{1,0:T(8,128)} async-done(((f32[1024,1024]{1,0:T(8,128)}), f32[1024,256]{1,0:T(8,128)}) %reduce-scatter.6.cloned.1.call-update) | async-done | bytes 1048592 | tf_op jit(solution)/shard_map/reduce_scatter | solution.py:183
  683.2 2.5 fusion.31
  685.7 47.4 %reduce-scatter.8.cloned.1.call-done = f32[3,128,256]{1,2,0:T(8,128)} async-done(((f32[3,1024,256]{1,2,0:T(8,128)}), f32[3,128,256]{1,2,0:T(8,128)}) %reduce-scatter.8.cloned.1.call-update) | async-done | bytes 393232 | tf_op jit(solution)/shard_map/reduce_scatter | solution.py:283
  733.0 1.9 copy.70
  735.0 38.1 %reduce-scatter.10.cloned.1.call-done = f32[256,128]{1,0:T(8,128)} async-done(((f32[256,1024]{1,0:T(8,128)}), f32[256,128]{1,0:T(8,128)}) %reduce-scatter.10.cloned.1.call-update) | async-done | bytes 131088 | tf_op jit(solution)/shard_map/reduce_scatter | solution.py:284
  773.0 55.6 %reduce-scatter.12.cloned.1.call-done = f32[128,1024]{1,0:T(8,128)} async-done(((f32[1024,1024]{1,0:T(8,128)}), f32[128,1024]{1,0:T(8,128)}) %reduce-scatter.12.cloned.1.call-update) | async-done | bytes 524304 | tf_op jit(solution)/shard_map/reduce_scatter | solution.py:285
  828.7 55.3 %reduce-scatter.14.cloned.1.call-done = f32[1024,128]{1,0:T(8,128)} async-done(((f32[1024,1024]{1,0:T(8,128)}), f32[1024,128]{1,0:T(8,128)}) %reduce-scatter.14.cloned.1.call-update) | async-done | bytes 524304 | tf_op jit(solution)/shard_map/reduce_scatter | solution.py:286
  (179 shorter events, 22.3 us)
Async XLA Ops:
  7.2 207.7 %copy-start = (bf16[1024,1024]{1,0:T(8,128)(2,1)S(1)}, bf16[1024,1024]{1,0:T(8,128)(2,1)}, u32[]{:S(2)}) copy-start(bf16[1024,1024]{1,0:T(8,128)(2,1)} %param.32) | copy-start | bytes 6291460
  7.2 5.1 copy-start.49
  7.3 5.9 copy-start.37
  7.3 6.5 copy-start.41
  7.3 6.5 copy-start.52
  7.3 6.5 copy-start.51
  7.3 198.5 %all-reduce.5.cloned.1.call-start = ((), (), s32[]{:S(2)}) async-start(), calls=%async_computation.5 | async-start | bytes 8388608 | tf_op jit(solution)/shard_map/psum | solution.py:175
  7.3 5.0 copy-start.21
  9.5 8.5 copy-start.34
  11.8 6.2 copy-start.32
  13.2 5.8 copy-start.29
  18.9 8.1 copy-start.13
  18.9 8.0 copy-start.6
  35.9 9.4 %copy-start.17 = (bf16[256,1024]{1,0:T(8,128)(2,1)S(1)}, bf16[256,1024]{1,0:T(8,128)(2,1)}, u32[]{:S(2)}) copy-start(bf16[256,1024]{1,0:T(8,128)(2,1)} %param.26) | copy-start | bytes 1572868
  48.0 157.9 %copy-start.40 = (f32[1024]{0:T(1024)S(1)}, f32[1024]{0:T(1024)}, u32[]{:S(2)}) copy-start(f32[1024]{0:T(1024)} %param.27) | copy-start | bytes 12292
  48.0 332.6 %all-reduce.7.cloned.1.call-start = ((), (), s32[]{:S(2)}) async-start(), calls=%async_computation.7 | async-start | bytes 8388608 | tf_op jit(solution)/shard_map/psum | solution.py:199
  209.3 5.6 copy-start.1
  209.4 176.5 %copy-start.30 = (f32[1024]{0:T(1024)}, f32[1024]{0:T(1024)S(1)}, u32[]{:S(2)}) copy-start(f32[1024]{0:T(1024)S(1)} %broadcast_multiply_fusion.5) | copy-start | bytes 12292
  212.4 173.4 %copy-start.35 = (f32[1024]{0:T(1024)}, f32[1024]{0:T(1024)S(1)}, u32[]{:S(2)}) copy-start(f32[1024]{0:T(1024)S(1)} %add_rsqrt_fusion) | copy-start | bytes 12292
  214.9 5.9 copy-start.58
  226.5 377.5 %all-reduce.9.cloned.1.call-start = ((), (), s32[]{:S(2)}) async-start(), calls=%async_computation.8 | async-start | bytes 8388608 | tf_op jit(solution)/shard_map/psum | solution.py:250
  380.6 5.3 copy-start.2
  380.6 5.9 copy-start.5
  386.6 5.7 copy-start.18
  419.3 12.7 %copy-start.26 = (f32[4,10,1024]{2,1,0:T(8,128)S(1)}, f32[4,10,1024]{2,1,0:T(8,128)}, u32[]{:S(2)}) copy-start(f32[4,10,1024]{2,1,0:T(8,128)} %get-tuple-element.170) | copy-start | bytes 491524
  419.3 12.7 %copy-start.7 = (bf16[1024,1,256]{0,2,1:T(8,128)(2,1)S(1)}, bf16[1024,1,256]{0,2,1:T(8,128)(2,1)}, u32[]{:S(2)}) copy-start(bf16[1024,1,256]{0,2,1:T(8,128)(2,1)} %copy-done.6) | copy-start | bytes 1572868
  432.1 5.1 copy-start.14
  437.2 7.1 copy-start.19
  444.3 5.5 copy-start.20
  449.9 233.3 %reduce-scatter.6.cloned.1.call-start = ((), (), s32[]{:S(2)}) async-start(), calls=%async_computation.6 | async-start | bytes 5242880 | tf_op jit(solution)/shard_map/reduce_scatter | solution.py:183
  457.4 6.0 copy-start.12
  457.5 275.6 %reduce-scatter.8.cloned.1.call-start = ((), (), s32[]{:S(2)}) async-start(), calls=%async_computation.9 | async-start | bytes 3538944 | tf_op jit(solution)/shard_map/reduce_scatter | solution.py:283
  463.4 309.6 %reduce-scatter.10.cloned.1.call-start = ((), (), s32[]{:S(2)}) async-start(), calls=%async_computation.10 | async-start | bytes 1179648 | tf_op jit(solution)/shard_map/reduce_scatter | solution.py:284
  467.6 361.1 %reduce-scatter.12.cloned.1.call-start = ((), (), s32[]{:S(2)}) async-start(), calls=%async_computation.11 | async-start | bytes 4718592 | tf_op jit(solution)/shard_map/reduce_scatter | solution.py:285
  475.3 408.6 %reduce-scatter.14.cloned.1.call-start = ((), (), s32[]{:S(2)}) async-start(), calls=%async_computation.12 | async-start | bytes 4718592 | tf_op jit(solution)/shard_map/reduce_scatter | solution.py:286
  483.8 6.7 copy-start.10
  483.8 7.1 copy-start.8
  492.9 117.3 %copy-start.43 = (f32[1024]{0:T(1024)S(1)}, f32[1024]{0:T(1024)}, u32[]{:S(2)}) copy-start(f32[1024]{0:T(1024)} %get-tuple-element.143) | copy-start | bytes 12292
  492.9 117.3 %copy-start.44 = (f32[256]{0:T(256)S(1)}, f32[256]{0:T(256)}, u32[]{:S(2)}) copy-start(f32[256]{0:T(256)} %dynamic_slice.67) | copy-start | bytes 3076
  492.9 117.3 %copy-start.45 = (f32[256]{0:T(256)S(1)}, f32[256]{0:T(256)}, u32[]{:S(2)}) copy-start(f32[256]{0:T(256)} %dynamic_slice.68) | copy-start | bytes 3076
  492.9 117.3 %copy-start.46 = (f32[256]{0:T(256)S(1)}, f32[256]{0:T(256)}, u32[]{:S(2)}) copy-start(f32[256]{0:T(256)} %dynamic_slice.66) | copy-start | bytes 3076
  492.9 117.3 %copy-start.47 = (f32[256]{0:T(256)S(1)}, f32[256]{0:T(256)}, u32[]{:S(2)}) copy-start(f32[256]{0:T(256)} %dynamic_slice.69) | copy-start | bytes 3076
  492.9 144.5 %copy-start.25 = (f32[10,512]{1,0:T(8,128)S(1)}, f32[10,512]{1,0:T(8,128)}, u32[]{:S(2)}) copy-start(f32[10,512]{1,0:T(8,128)} %copy-done.24) | copy-start | bytes 61444
  492.9 146.4 %copy-start.22 = (bf16[512,2,256]{2,1,0:T(2,128)(2,1)S(1)}, bf16[512,2,256]{2,1,0:T(2,128)(2,1)}, u32[]{:S(2)}) copy-start(bf16[512,2,256]{2,1,0:T(2,128)(2,1)} %param.37) | copy-start | bytes 1572868
  492.9 165.3 %copy-start.28 = (f32[10,1024]{1,0:T(8,128)S(1)}, f32[10,1024]{1,0:T(8,128)}, u32[]{:S(2)}) copy-start(f32[10,1024]{1,0:T(8,128)} %param.34) | copy-start | bytes 122884
  637.5 27.6 %copy-start.33 = (f32[1024]{0:T(1024)S(1)}, f32[1024]{0:T(1024)}, u32[]{:S(2)}) copy-start(f32[1024]{0:T(1024)} %copy-done.32) | copy-start | bytes 12292
  661.5 6.8 copy-start.16
  661.5 21.6 %copy-start.42 = (f32[256]{0:T(256)S(1)}, f32[256]{0:T(256)}, u32[]{:S(2)}) copy-start(f32[256]{0:T(256)} %dynamic-slice.5) | copy-start | bytes 3076
  (20 other events, 53.2 us)
Sparse Core Ops, SparseCore 0:
  48.1 157.6 all-reduce.4
  226.6 153.9 all-reduce.6
  450.0 153.9 all-reduce.8
  606.3 76.8 reduce-scatter.5
  686.4 46.6 reduce-scatter.7
  737.0 36.0 reduce-scatter.9
  777.3 51.2 reduce-scatter.11
  832.6 51.2 reduce-scatter.13
where the time goes:
time: 896 us; the launch traced here: 891 us
  waiting for transfers between devices  633 us (71%)
  matrix products  115 us (13%)
  other arithmetic  54.3 us (6%)
  blocking collectives  45.1 us (5%)
  local copies, waits for them, and re-layouts  28.2 us (3%)
  between operations  15.1 us (2%)
    psum x1, waiting for transfers between devices, shards(): lax.psum(jnp.dot(attended, output_weight, preferred_element_type=jnp.floa...  158 us
    psum x1, waiting for transfers between devices, shards(): lax.psum(jnp.einsum('tf,df->td', grad_pre, up_weight, preferred_element_t...  154 us
    psum x1, waiting for transfers between devices, shards(): grad_attention = lax.psum(grad_attention_part, 'tensor')  111 us
    reduce_scatter x1, waiting for transfers between devices, shards(): lax.psum_scatter(up_gradient, 'batch', scatter_dimension=0, tiled=True)  55.6 us
    reduce_scatter x1, waiting for transfers between devices, shards(): lax.psum_scatter(down_gradient, 'batch', scatter_dimension=1, tiled=True)  55.3 us
    reduce_scatter x1, waiting for transfers between devices, shards(): lax.psum_scatter(joint_gradient, 'batch', scatter_dimension=1, tiled=True)  47.4 us
    reduce_scatter x1, waiting for transfers between devices, shards(): lax.psum_scatter(output_gradient, 'batch', scatter_dimension=1, tiled=True)  38.1 us
    psum x1, blocking collectives, shards(): lax.psum((joint_bias_sum, up_bias_sum, attention_gain_sum, attention_shif...  26.6 us
  transfers between devices with their start and end apart: 8, of which 8 were waited for; matrix products, arithmetic and copies ran while one was open for 7% of the time, Pallas kernels for 0%

commit v1 on v0

v1 whole, which is shorter than its diff:
```python
import functools

import jax
import jax.numpy as jnp
from jax import lax
from jax.experimental import pallas as pl
from jax.experimental.pallas import tpu as pltpu
from jax.sharding import PartitionSpec as P

HD = 64
GROUP = 4
WIDE = GROUP * HD
QB = 256
PAD = 16
TB = 256
EPSILON = 1e-05
PRECISE = lax.Precision.HIGHEST
NEGATIVE = -1e30
VMEM = 56 * 2**20
F32, BF16 = jnp.float32, jnp.bfloat16
NN = (((1,), (0,)), ((), ()))
NT = (((1,), (1,)), ((), ()))
TN = (((0,), (0,)), ((), ()))
TT = (((0,), (1,)), ((), ()))
shape_of = jax.ShapeDtypeStruct


def dot(a, b, dims=NN):
    return lax.dot_general(a, b, dims, preferred_element_type=F32)


def params(**kw):
    return pltpu.CompilerParams(vmem_limit_bytes=VMEM, **kw)


def normalize(values):
    centered = values - jnp.mean(values, axis=-1, keepdims=True)
    inverse = lax.rsqrt(jnp.mean(centered * centered, axis=-1, keepdims=True) + EPSILON)
    return centered * inverse, inverse


def heads_kernel(turn, member_ref, joint_ref, out_ref, own_ref, send_ref):
    for c in range(3):
        own_ref[c] = joint_ref[c].T
    own_ref[3] = out_ref[...]
    rows = own_ref.shape[1] // 8
    for p in range(2):
        member = member_ref[0] ^ (turn * p)
        start = pl.multiple_of(member * rows, rows)
        for c in range(4):
            send_ref[p, c * rows : (c + 1) * rows, :] = own_ref[c, pl.ds(start, rows), :].astype(F32)


def head_pieces(member, joint_weight, output_weight):
    _, width, local = joint_weight.shape
    vm = pl.BlockSpec(memory_space=pltpu.VMEM)
    return pl.pallas_call(
        functools.partial(heads_kernel, 6),
        out_shape=[shape_of((4, local, width), BF16), shape_of((2, local // 2, width), F32)],
        in_specs=[pl.BlockSpec(memory_space=pltpu.SMEM), vm, vm],
        out_specs=[vm, vm],
        compiler_params=params(),
        name="head_pieces",
    )(member, joint_weight, output_weight)


def hidden_kernel(member_ref, up_ref, down_ref, send_ref):
    rows = down_ref.shape[0]
    send_ref[0, 0:rows, :] = up_ref[...].T.astype(F32)
    send_ref[0, rows : 2 * rows, :] = down_ref[...].astype(F32)


def hidden_pieces(member, up_weight, down_weight):
    width, local = up_weight.shape
    rows = local // 8
    return pl.pallas_call(
        hidden_kernel,
        out_shape=shape_of((2, 2 * rows, width), F32),
        grid_spec=pltpu.PrefetchScalarGridSpec(
            num_scalar_prefetch=1,
            grid=(2,),
            in_specs=[
                pl.BlockSpec((width, rows), lambda p, m: (0, m[0] ^ (6 * p))),
                pl.BlockSpec((rows, width), lambda p, m: (m[0] ^ (6 * p), 0)),
            ],
            out_specs=pl.BlockSpec((1, 2 * rows, width), lambda p, m: (p, 0, 0)),
        ),
        compiler_params=params(),
        name="hidden_pieces",
    )(member, up_weight, down_weight)


def head_of_lane(rows):
    return lax.broadcasted_iota(jnp.int32, (rows, WIDE), 1) // HD


def first_key(i, length):
    return max(0, (i * QB - length // 2 + 1) // QB) * QB


def mask_tile(seg_col, seg_row, first, last, start):
    keys = lax.broadcasted_iota(jnp.int32, (last - first, QB), 0) + first
    asks = lax.broadcasted_iota(jnp.int32, (last - first, QB), 1) + start
    allowed = (seg_col == seg_row) & (keys <= asks)
    return jnp.where(allowed, 0.0, NEGATIVE)


def attend_kernel(merge, prefix_count, *refs):
    if merge:
        x_ref, mine_ref, theirs_ref, bias_ref, pk_ref, pv_ref, segc_ref, segr_ref, acc_ref = refs[:9]
        w_ref, q_ref, k_ref, v_ref, att_ref, lse_ref, out_ref, mask_ref, vt_ref = refs[9:]
        half = HD // 2
        for g in range(GROUP):
            for c in range(4):
                piece = slice(g * 4 * half + c * half, g * 4 * half + (c + 1) * half)
                w_ref[c, g * HD : g * HD + half, :] = mine_ref[piece, :].astype(BF16)
                w_ref[c, g * HD + half : (g + 1) * HD, :] = theirs_ref[piece, :].astype(BF16)
    else:
        tok_ref, gain_ref, shift_ref, w_ref, bias_ref, pk_ref, pv_ref, segc_ref, segr_ref, acc_ref = refs[:10]
        x_ref, q_ref, k_ref, v_ref, att_ref, lse_ref, out_ref, mask_ref, vt_ref = refs[10:]
        for t in range(0, tok_ref.shape[0], TB):
            normed, _ = normalize(tok_ref[t : t + TB, :].astype(F32))
            x_ref[t : t + TB, :] = (normed * gain_ref[...] + shift_ref[...]).astype(BF16)
    length = x_ref.shape[0]
    x = x_ref[...]
    q_ref[...] = ((dot(x, w_ref[0], NT) + bias_ref[0:1, :]) * HD ** (-0.5)).astype(BF16)
    k_ref[...] = (dot(x, w_ref[1], NT) + bias_ref[1:2, :]).astype(BF16)
    v_ref[...] = (dot(x, w_ref[2], NT) + bias_ref[2:3, :]).astype(BF16)
    vt_ref[...] = v_ref[...].T
    pvt = pv_ref[...].astype(BF16).T
    pk = pk_ref[...].astype(BF16)
    live = lax.broadcasted_iota(jnp.int32, (PAD, QB), 0) < prefix_count
    heads = head_of_lane(QB)
    for i in range(length // QB):
        first, last, rows = first_key(i, length), (i + 1) * QB, slice(i * QB, (i + 1) * QB)
        mask_ref[first:last, :] = mask_tile(segc_ref[first:last, :], segr_ref[:, rows], first, last, i * QB)
        for h in range(GROUP):
            span = slice(h * HD, (h + 1) * HD)
            asked = jnp.where(heads == h, q_ref[rows, :], jnp.zeros((), BF16))
            s = dot(k_ref[first:last, :], asked, NT) + mask_ref[first:last, :]
            sp = jnp.where(live, dot(pk, asked, NT), NEGATIVE)
            top = jnp.maximum(jnp.max(s, axis=0, keepdims=True), jnp.max(sp, axis=0, keepdims=True))
            e, ep = jnp.exp(s - top), jnp.exp(sp - top)
            total = jnp.sum(e, axis=0, keepdims=True) + jnp.sum(ep, axis=0, keepdims=True)
            o = dot(vt_ref[span, first:last], e.astype(BF16)) + dot(pvt[span, :], ep.astype(BF16))
            att_ref[span, rows] = (o / total).astype(BF16)
            lse_ref[h : h + 1, rows] = top + jnp.log(total)
    if merge:
        out_ref[...] = acc_ref[...] + dot(att_ref[...], w_ref[3], TN)
    else:
        for t in range(0, length, TB):
            base = tok_ref[t : t + TB, :].astype(F32) + acc_ref[...]
            out_ref[t : t + TB, :] = base + dot(att_ref[:, t : t + TB], w_ref[3], TN)


def attend_outs(length, width):
    return [shape_of((length, WIDE), BF16)] * 3 + [
        shape_of((WIDE, length), BF16),
        shape_of((GROUP, length), F32),
        shape_of((length, width), F32),
    ]


def attend(merge, prefix_count, length, width, args):
    first = shape_of((4, WIDE, width), BF16) if merge else shape_of((length, width), BF16)
    return pl.pallas_call(
        functools.partial(attend_kernel, merge, prefix_count),
        out_shape=[first] + attend_outs(length, width),
        scratch_shapes=[pltpu.VMEM((length, QB), F32), pltpu.VMEM((WIDE, length), BF16)],
        compiler_params=params(),
        name="attend_others" if merge else "attend_own",
    )(*args)


def back_kernel(own, prefix_count, own_start, *refs):
    w_ref, q_ref, k_ref, v_ref, att_ref, lse_ref, pk_ref, pv_ref, segc_ref, segr_ref, gr_ref = refs[:11]
    if own:
        gj_ref, gp_ref, out_ref, mask_ref, kt_ref, p_ref, ds_ref, do_ref, dot_ref, dqt_ref, dk_ref, dv_ref, qm_ref, gm_ref = refs[11:]
    else:
        acc_ref, out_ref, mask_ref, kt_ref, p_ref, ds_ref, do_ref, dot_ref, dqt_ref, dk_ref, dv_ref, qm_ref, gm_ref, gj_ref = refs[11:]
    length = q_ref.shape[0]
    do_ref[...] = dot(gr_ref[...], w_ref[3], NT).astype(BF16)
    dot_ref[...] = do_ref[...].T
    kt_ref[...] = k_ref[...].T
    pk, pv = pk_ref[...].astype(BF16), pv_ref[...].astype(BF16)
    pkt = pk.T
    live = lax.broadcasted_iota(jnp.int32, (PAD, QB), 0) < prefix_count
    heads = head_of_lane(QB)
    dk_ref[...] = jnp.zeros_like(dk_ref)
    dv_ref[...] = jnp.zeros_like(dv_ref)
    zero = jnp.zeros((), BF16)
    gpk = jnp.zeros((PAD, WIDE), F32)
    gpv = jnp.zeros((PAD, WIDE), F32)
    for i in range(length // QB):
        first, last, rows = first_key(i, length), (i + 1) * QB, slice(i * QB, (i + 1) * QB)
        mask_ref[first:last, :] = mask_tile(segc_ref[first:last, :], segr_ref[:, rows], first, last, i * QB)
        for h in range(GROUP):
            span, lanes = slice(h * HD, (h + 1) * HD), slice(h * QB, (h + 1) * QB)
            asked = jnp.where(heads == h, q_ref[rows, :], zero)
            grad = jnp.where(heads == h, do_ref[rows, :], zero)
            qm_ref[lanes, :] = asked
            gm_ref[lanes, :] = grad
            lse = lse_ref[h : h + 1, rows]
            delta = jnp.sum(dot_ref[span, rows].astype(F32) * att_ref[span, rows].astype(F32), axis=0, keepdims=True)
            p = jnp.exp(dot(k_ref[first:last, :], asked, NT) + mask_ref[first:last, :] - lse)
            p_ref[first:last, lanes] = p.astype(BF16)
            ds = (p * (dot(v_ref[first:last, :], grad, NT) - delta)).astype(BF16)
            ds_ref[first:last, lanes] = ds
            pp = jnp.exp(jnp.where(live, dot(pk, asked, NT), NEGATIVE) - lse)
            dsp = (pp * (dot(pv, grad, NT) - delta)).astype(BF16)
            dqt_ref[span, rows] = dot(kt_ref[span, first:last], ds) + dot(pkt[span, :], dsp)
            if own:
                gpk = gpk + dot(dsp, asked)
                gpv = gpv + dot(pp.astype(BF16), grad)
        dk_ref[first:last, :] += dot(ds_ref[first:last, :], qm_ref[...])
        dv_ref[first:last, :] += dot(p_ref[first:last, :], gm_ref[...])
    gj_ref[:, 0:WIDE] = dqt_ref[...].astype(BF16).T * jnp.asarray(HD ** (-0.5), BF16)
    gj_ref[:, WIDE : 2 * WIDE] = dk_ref[...].astype(BF16)
    gj_ref[:, 2 * WIDE : 3 * WIDE] = dv_ref[...].astype(BF16)
    part = dot(gj_ref[...], w_ref[0:3].reshape(3 * WIDE, w_ref.shape[2]))
    if own:
        gp_ref[0] = gpk
        gp_ref[1] = gpv
        out_ref[...] = part
    else:
        out_ref[...] = acc_ref[...] + part


def attend_back(own, prefix_count, args):
    length, width = args[10].shape
    outs = [shape_of((length, width), F32)]
    scratch = [
        pltpu.VMEM((length, QB), F32),
        pltpu.VMEM((WIDE, length), BF16),
        pltpu.VMEM((length, GROUP * QB), BF16),
        pltpu.VMEM((length, GROUP * QB), BF16),
        pltpu.VMEM((length, WIDE), BF16),
        pltpu.VMEM((WIDE, length), BF16),
        pltpu.VMEM((WIDE, length), F32),
        pltpu.VMEM((length, WIDE), F32),
        pltpu.VMEM((length, WIDE), F32),
        pltpu.VMEM((GROUP * QB, WIDE), BF16),
        pltpu.VMEM((GROUP * QB, WIDE), BF16),
    ]
    if own:
        outs = [shape_of((length, 3 * WIDE), BF16), shape_of((2, PAD, WIDE), F32)] + outs
    else:
        scratch = scratch + [pltpu.VMEM((length, 3 * WIDE), BF16)]
    return pl.pallas_call(
        functools.partial(back_kernel, own, prefix_count, 0),
        out_shape=outs,
        scratch_shapes=scratch,
        compiler_params=params(),
        name="back_own" if own else "back_others",
    )(*args)


def gelu_pair(v):
    c = 0.7978845608028654
    t = jnp.tanh(c * (v + 0.044715 * (v * v * v)))
    half = 0.5 * (1.0 + t)
    return v * half, half + 0.5 * v * (1.0 - t * t) * (c + (3.0 * 0.044715 * c) * (v * v))


def mix_own_kernel(z_ref, res_ref, cot_ref, gain_ref, shift_ref, up_ref, bias_ref, down_ref, dbias_ref,
                   mid_ref, act_ref, gp_ref, share_ref, gm_ref, bsum_ref):
    start = pl.multiple_of(z_ref[0] * share_ref.shape[1], share_ref.shape[1])
    own = pl.ds(start, share_ref.shape[1])
    normed, _ = normalize(res_ref[...])
    mid = (normed * gain_ref[...] + shift_ref[...]).astype(BF16)
    mid_ref[...] = mid
    act, slope = gelu_pair(dot(mid, up_ref[...]) + bias_ref[...])
    act = act.astype(BF16)
    act_ref[...] = act
    gp = (dot(cot_ref[...], down_ref[...], NT) * slope).astype(BF16)
    gp_ref[...] = gp
    share_ref[...] = res_ref[:, own] + dbias_ref[:, own] + dot(act, down_ref[:, own])
    gm_ref[...] = dot(gp, up_ref[...], NT)

    @pl.when(pl.program_id(0) == 0)
    def _():
        bsum_ref[...] = jnp.zeros_like(bsum_ref)

    bsum_ref[...] += jnp.sum(gp.astype(F32), axis=0, keepdims=True)


def mix_own(z, residual, cotangent, gain, shift, up, up_bias, down, down_bias, own_width):
    length, width = residual.shape
    hidden = up.shape[1]
    rows = lambda w: pl.BlockSpec((TB, w), lambda t: (t, 0))
    whole = lambda a: pl.BlockSpec(a.shape, lambda t: (0, 0), pipeline_mode=pl.Buffered(1))
    return pl.pallas_call(
        mix_own_kernel,
        grid=(length // TB,),
        in_specs=[
            pl.BlockSpec(memory_space=pltpu.SMEM),
            rows(width),
            rows(width),
            whole(gain),
            whole(shift),
            whole(up),
            whole(up_bias),
            whole(down),
            whole(down_bias),
        ],
        out_specs=[rows(width), rows(hidden), rows(hidden), rows(own_width), rows(width), pl.BlockSpec((1, hidden), lambda t: (0, 0))],
        out_shape=[
            shape_of((length, width), BF16),
            shape_of((length, hidden), BF16),
            shape_of((length, hidden), BF16),
            shape_of((length, own_width), F32),
            shape_of((length, width), F32),
            shape_of((1, hidden), F32),
        ],
        compiler_params=params(),
        name="mix_own",
    )(z, residual, cotangent, gain, shift, up, up_bias, down, down_bias)


def mix_kernel(pieces, z_ref, mid_ref, cot_ref, mine_ref, theirs_ref, bias_ref, share_in, gm_in, share_ref, gm_ref, up_ref, down_ref, part_ref):
    rows = mine_ref.shape[0] // pieces // 2
    start = pl.multiple_of(z_ref[0] * share_ref.shape[1], share_ref.shape[1])
    own = pl.ds(start, share_ref.shape[1])

    @pl.when(pl.program_id(0) == 0)
    def _():
        for g in range(pieces):
            for side, ref in enumerate((mine_ref, theirs_ref)):
                to = slice((2 * g + side) * rows, (2 * g + side + 1) * rows)
                up_ref[to, :] = ref[2 * g * rows : (2 * g + 1) * rows, :].astype(BF16)
                down_ref[to, :] = ref[(2 * g + 1) * rows : (2 * g + 2) * rows, :].astype(BF16)
        part_ref[...] = down_ref[:, own]

    mid = mid_ref[...]
    act, slope = gelu_pair(dot(mid, up_ref[...], NT) + bias_ref[...])
    gp = (dot(cot_ref[...], down_ref[...], NT) * slope).astype(BF16)
    share_ref[...] = (share_in[...] + dot(act.astype(BF16), part_ref[...])).astype(share_ref.dtype)
    gm_ref[...] = gm_in[...] + dot(gp, up_ref[...])


def mix(z, mid, cotangent, mine, theirs, bias, share, gm, last):
    length, width = mid.shape
    pieces = 4
    hidden = mine.shape[0]
    own_width = share.shape[1]
    rows = lambda w: pl.BlockSpec((TB, w), lambda t: (t, 0))
    whole = lambda a: pl.BlockSpec(a.shape, lambda t: (0, 0), pipeline_mode=pl.Buffered(1))
    return pl.pallas_call(
        functools.partial(mix_kernel, pieces),
        grid=(length // TB,),
        in_specs=[
            pl.BlockSpec(memory_space=pltpu.SMEM),
            rows(width),
            rows(width),
            whole(mine),
            whole(theirs),
            whole(bias),
            rows(own_width),
            rows(width),
        ],
        out_specs=[rows(own_width), rows(width)],
        out_shape=[shape_of((length, own_width), BF16 if last else F32), shape_of((length, width), F32)],
        scratch_shapes=[pltpu.VMEM((hidden, width), BF16), pltpu.VMEM((hidden, width), BF16), pltpu.VMEM((hidden, own_width), BF16)],
        compiler_params=params(),
        name="mix_others",
    )(z, mid, cotangent, mine, theirs, bias, share, gm)


def residual_kernel(z_ref, res_ref, cot_ref, gm_ref, gain_ref, low_ref, part_ref, sums_ref):
    start = pl.multiple_of(z_ref[0] * part_ref.shape[1], part_ref.shape[1])
    normed, inverse = normalize(res_ref[...])
    gm = gm_ref[...]
    cot = cot_ref[...].astype(F32)
    scaled = gm * gain_ref[...]
    grad = cot + inverse * (
        scaled - jnp.mean(scaled, axis=-1, keepdims=True) - normed * jnp.mean(scaled * normed, axis=-1, keepdims=True)
    )
    low_ref[...] = grad.astype(BF16)

    @pl.when(pl.program_id(0) == 0)
    def _():
        sums_ref[...] = jnp.zeros_like(sums_ref)

    sums_ref[0:1, :] += jnp.sum(gm * normed, axis=0, keepdims=True)
    sums_ref[1:2, :] += jnp.sum(gm, axis=0, keepdims=True)
    sums_ref[2:3, :] += jnp.sum(grad, axis=0, keepdims=True)
    sums_ref[3:4, :] += jnp.sum(cot, axis=0, keepdims=True)
    grid_own(part_ref, grad, z_ref[0])


def grid_own(part_ref, values, index):
    width = part_ref.shape[1]
    for k in range(values.shape[1] // width):

        @pl.when(index == k)
        def _():
            part_ref[...] = values[:, k * width : (k + 1) * width].astype(part_ref.dtype)


def residual_back(z, residual, cotangent, gm, gain, own_width):
    length, width = residual.shape
    rows = lambda w: pl.BlockSpec((TB, w), lambda t: (t, 0))
    return pl.pallas_call(
        residual_kernel,
        grid=(length // TB,),
        in_specs=[
            pl.BlockSpec(memory_space=pltpu.SMEM),
            rows(width),
            rows(width),
            rows(width),
            pl.BlockSpec((1, width), lambda t: (0, 0)),
        ],
        out_specs=[rows(width), rows(own_width), pl.BlockSpec((8, width), lambda t: (0, 0))],
        out_shape=[shape_of((length, width), BF16), shape_of((length, own_width), F32), shape_of((8, width), F32)],
        compiler_params=params(),
        name="residual_back",
    )(z, residual, cotangent, gm, gain)


def final_kernel(z_ref, tok_ref, part_ref, ga_ref, gain_ref, out_ref, sums_ref):
    normed, inverse = normalize(tok_ref[...].astype(F32))
    ga = ga_ref[...]
    scaled = ga * gain_ref[...]
    grad = inverse * (
        scaled - jnp.mean(scaled, axis=-1, keepdims=True) - normed * jnp.mean(scaled * normed, axis=-1, keepdims=True)
    )
    width = out_ref.shape[1]

    @pl.when(pl.program_id(0) == 0)
    def _():
        sums_ref[...] = jnp.zeros_like(sums_ref)

    for k in range(grad.shape[1] // width):

        @pl.when(z_ref[0] == k)
        def _():
            own = slice(k * width, (k + 1) * width)
            out_ref[...] = (part_ref[...] + grad[:, own]).astype(BF16)
            sums_ref[0:1, :] += jnp.sum(ga[:, own] * normed[:, own], axis=0, keepdims=True)
            sums_ref[1:2, :] += jnp.sum(ga[:, own], axis=0, keepdims=True)


def final_back(z, tokens, part, ga, gain):
    length, width = tokens.shape
    own_width = part.shape[1]
    rows = lambda w: pl.BlockSpec((TB, w), lambda t: (t, 0))
    return pl.pallas_call(
        final_kernel,
        grid=(length // TB,),
        in_specs=[
            pl.BlockSpec(memory_space=pltpu.SMEM),
            rows(width),
            rows(own_width),
            rows(width),
            pl.BlockSpec((1, width), lambda t: (0, 0)),
        ],
        out_specs=[rows(own_width), pl.BlockSpec((8, own_width), lambda t: (0, 0))],
        out_shape=[shape_of((length, own_width), BF16), shape_of((8, own_width), F32)],
        compiler_params=params(),
        name="final_back",
    )(z, tokens, part, ga, gain)


def hidden_grad_kernel(mid_ref, cot_ref, gp_ref, act_ref, out_ref):
    parts, per = out_ref.shape[0], out_ref.shape[1] // 2
    for at, left, right in ((0, mid_ref, gp_ref), (per, cot_ref, act_ref)):
        grad = dot(left[...], right[...], TN)
        for a in range(parts):
            out_ref[a, at : at + per, :] = grad[a * per : (a + 1) * per]


def hidden_grad(mid, cotangent, gp, act, parts):
    length, width = mid.shape
    hidden = gp.shape[1]
    rows = 128
    per = width // parts
    column = pl.BlockSpec((length, rows), lambda j: (0, j))
    whole = pl.BlockSpec((length, hidden), lambda j: (0, 0), pipeline_mode=pl.Buffered(1))
    return pl.pallas_call(
        hidden_grad_kernel,
        grid=(width // rows,),
        in_specs=[column, column, whole, whole],
        out_specs=pl.BlockSpec((rows // per, 2 * per, hidden), lambda j: (j, 0, 0)),
        out_shape=shape_of((parts, 2 * per, hidden), F32),
        compiler_params=params(),
        name="hidden_grad",
    )(mid, cotangent, gp, act)


def head_grad_kernel(x_ref, low_ref, gj_ref, att_ref, out_ref, bsum_ref):
    wide = gj_ref.shape[1]
    out_ref[0, :, 0:wide] = dot(x_ref[...], gj_ref[...], TN)
    out_ref[0, :, wide:] = dot(low_ref[...], att_ref[...], TT)

    @pl.when(pl.program_id(0) == 0)
    def _():
        bsum_ref[...] = jnp.sum(gj_ref[...].astype(F32), axis=0, keepdims=True)


def head_grad(x, low, gj, att):
    length, width = x.shape
    wide, local = gj.shape[1], att.shape[0]
    rows = 128
    column = pl.BlockSpec((length, rows), lambda j: (0, j))
    whole = lambda a: pl.BlockSpec(a.shape, lambda j: (0, 0), pipeline_mode=pl.Buffered(1))
    return pl.pallas_call(
        head_grad_kernel,
        grid=(width // rows,),
        in_specs=[column, column, whole(gj), whole(att)],
        out_specs=[pl.BlockSpec((1, rows, wide + local), lambda j: (j, 0, 0)), pl.BlockSpec((1, wide), lambda j: (0, 0))],
        out_shape=[shape_of((width // rows, rows, wide + local), F32), shape_of((1, wide), F32)],
        compiler_params=params(),
        name="head_grad",
    )(x, low, gj, att)


def shards(
    tokens, segment_ids, attention_gain, attention_shift, joint_weight, joint_bias, output_weight, output_bias,
    mixer_gain, mixer_shift, up_weight, up_bias, down_weight, down_bias, prefix_table, inner_weight, inner_bias,
    outer_weight, outer_bias, cotangent,
):
    length, width = tokens.shape
    local = joint_weight.shape[2]
    hidden = up_weight.shape[1]
    prefix_count = prefix_table.shape[0]
    batch_size, tensor_size = lax.axis_size("batch"), lax.axis_size("tensor")
    z = lax.axis_index("tensor").astype(jnp.int32)
    member = (lax.axis_index("batch") % 8).astype(jnp.int32)
    z_arr, member_arr = z.reshape(1), member.reshape(1)

    def own_columns(values):
        return lax.dynamic_slice_in_dim(values, z * local, local, values.ndim - 1)

    def along(values, k):
        return lax.ppermute(values, "tensor", [(i, i ^ k) for i in range(tensor_size)])

    def across(values, k):
        return lax.ppermute(values, "batch", [(i, i ^ k) for i in range(batch_size)])

    row = lambda v: v.reshape(1, -1)
    own_heads, send_heads = head_pieces(member_arr, joint_weight, output_weight)
    send_hidden = hidden_pieces(member_arr, up_weight, down_weight)

    hidden_prefix = jnp.tanh(jnp.dot(prefix_table, inner_weight.astype(F32), precision=PRECISE) + inner_bias)
    outer_float = outer_weight.astype(F32)
    prefix_pairs = jnp.einsum("pr,rke->kpe", hidden_prefix, outer_float, precision=PRECISE) + outer_bias[:, None, :]
    prefix_padded = jnp.pad(prefix_pairs, ((0, 0), (0, PAD - prefix_count), (0, 0)))

    small = jnp.concatenate([prefix_padded.reshape(2 * PAD, local), joint_bias, up_bias.reshape(8, hidden // 256, 32).transpose(1, 0, 2).reshape(-1, local), jnp.zeros((1, local), F32)], axis=0)

    def reorder(values):
        parts = values.reshape(values.shape[0], 8, local // 8)
        for bit in (1, 2, 4):
            turned = parts.reshape(values.shape[0], 4 // bit, 2, bit, local // 8)[:, :, ::-1].reshape(parts.shape)
            parts = jnp.where((member & bit) > 0, turned, parts)
        return parts.reshape(values.shape)

    smalls = [reorder(along(small, k)) for k in (1, 2, 3)]

    def plane(first, diagonal, turn):
        x1, y1 = across(first, 2), across(first, 4)
        if diagonal is None:
            diagonal = across(x1, 4) if turn == 2 else across(y1, 2)
        mine = jnp.concatenate([first, x1, y1, diagonal], axis=0)
        return mine, across(mine, 1)

    def slots(send):
        return [
            plane(along(send[0], 1), along(send[1], 1), 1),
            plane(along(send[0], 2), None, 2),
            plane(along(send[0], 3), None, 3),
        ]

    seg_row = segment_ids
    seg_col = segment_ids.reshape(length, 1)
    others = slots(send_heads)
    x, *saved, residual = attend(
        False, prefix_count, length, width,
        (tokens, row(attention_gain), row(attention_shift), own_heads, joint_bias, prefix_padded[0], prefix_padded[1], seg_col, seg_row, row(output_bias)),
    )
    groups = [(own_heads, saved, prefix_padded[0], prefix_padded[1])]
    for (mine, theirs), extra in zip(others, smalls):
        pk, pv, bias = extra[0:PAD], extra[PAD : 2 * PAD], extra[2 * PAD : 2 * PAD + 3]
        w, *saved, residual = attend(True, prefix_count, length, width, (x, mine, theirs, bias, pk, pv, seg_col, seg_row, residual))
        groups.append((w, saved, pk, pv))

    mid, act, gp, share, gm, up_bias_sum = mix_own(
        z_arr, residual, cotangent, row(mixer_gain), row(mixer_shift), up_weight, row(up_bias), down_weight, row(down_bias), local
    )
    hidden_sum = lax.psum_scatter(hidden_grad(mid, cotangent, gp, act, batch_size), "batch", scatter_dimension=0, tiled=False)
    for k, ((mine, theirs), extra) in enumerate(zip(slots(send_hidden), smalls)):
        bias = extra[2 * PAD + 3 : 2 * PAD + 3 + hidden // 256].reshape(hidden // 256, 8, 32).transpose(1, 0, 2).reshape(1, hidden)
        share, gm = mix(z_arr, mid, cotangent, mine, theirs, bias, share, gm, k == 2)
    low, part, sums = residual_back(z_arr, residual, cotangent, gm, row(mixer_gain), local)

    w, saved, pk, pv = groups[0]
    gj, gprefix, ga = attend_back(True, prefix_count, (w, *saved, pk, pv, seg_col, seg_row, low))
    head_parts, joint_bias_sum = head_grad(x, low, gj, saved[3])
    head_sum = lax.psum_scatter(head_parts.reshape(batch_size, -1, 3 * local + local), "batch", scatter_dimension=0, tiled=False)
    gprefix = gprefix[:, :prefix_count]
    grad_hidden_part = jnp.einsum("kpe,rke->pr", gprefix, outer_float, precision=PRECISE)
    for w, saved, pk, pv in groups[1:]:
        (ga,) = attend_back(False, prefix_count, (w, *saved, pk, pv, seg_col, seg_row, low, ga))
    tokens_gradient, gain_sums = final_back(z_arr, tokens, part, ga, row(attention_gain))

    mixed = own_columns(sums[0:4])
    totals = lax.psum((joint_bias_sum, up_bias_sum, mixed, gain_sums[0:2], gprefix), "batch")
    grad_hidden_prefix = lax.psum(grad_hidden_part, ("batch", "tensor"))
    joint_bias_total, up_bias_total, mixed_total, gain_total, grad_prefix = totals
    outer_rows = outer_weight.shape[0] // batch_size
    hidden_own = lax.dynamic_slice_in_dim(hidden_prefix, lax.axis_index("batch") * outer_rows, outer_rows, 1)
    outer_total = jnp.einsum("pr,kpe->rke", hidden_own, grad_prefix, precision=PRECISE)
    outer_bias_total = jnp.sum(grad_prefix, axis=1)
    grad_inner = grad_hidden_prefix * (1.0 - hidden_prefix * hidden_prefix)
    inner_total = jnp.einsum("pd,pr->dr", prefix_table, grad_inner, precision=PRECISE)
    inner_bias_total = jnp.sum(grad_inner, axis=0)
    table_total = jnp.einsum("pr,dr->pd", grad_inner, inner_weight.astype(F32), precision=PRECISE)

    per = width // batch_size
    up_total, down_total = hidden_sum[:per], hidden_sum[per:].T
    head_sum = head_sum.reshape(per, 4 * local)
    joint_total = head_sum[:, : 3 * local].reshape(per, 3, local).transpose(1, 0, 2)
    output_total = head_sum[:, 3 * local :].T
    return (
        share,
        tokens_gradient,
        gain_total[0],
        gain_total[1],
        joint_total,
        joint_bias_total.reshape(3, local),
        output_total,
        mixed_total[2],
        mixed_total[0],
        mixed_total[1],
        up_total,
        up_bias_total.reshape(hidden),
        down_total,
        mixed_total[3],
        table_total,
        inner_total,
        inner_bias_total,
        outer_total,
        outer_bias_total,
    )


def solution(mesh):
    placed = (
        P("batch", None),
        P("batch", None),
        P(),
        P(),
        P(None, None, "tensor"),
        P(None, "tensor"),
        P("tensor", None),
        P(),
        P(),
        P(),
        P(None, "tensor"),
        P("tensor"),
        P("tensor", None),
        P(),
        P(),
        P(),
        P(),
        P(None, None, "tensor"),
        P(None, "tensor"),
        P("batch", None),
    )
    return jax.shard_map(
        shards,
        mesh=mesh,
        in_specs=placed,
        out_specs=(
            P("batch", "tensor"),
            P("batch", "tensor"),
            P("tensor"),
            P("tensor"),
            P(None, "batch", "tensor"),
            P(None, "tensor"),
            P("tensor", "batch"),
            P("tensor"),
            P("tensor"),
            P("tensor"),
            P("batch", "tensor"),
            P("tensor"),
            P("tensor", "batch"),
            P("tensor"),
            P(),
            P(),
            P(),
            P("batch", None, "tensor"),
            P(None, "tensor"),
        ),
        check_vma=False,
    )
```

time: 896 us -> 651 us (0.73)
  waiting for transfers between devices: 633 us -> 198 us
  Pallas kernels: 0 us -> 237 us
  matrix products: 115 us -> 5.14 us
  local copies, waits for them, and re-layouts: 28.2 us -> 78 us
  other arithmetic: 54.3 us -> 5.54 us
  starting transfers between devices: 0.5 us -> 37.8 us
  blocking collectives: 45.1 us -> 63.1 us
    psum x3 -> x0, waiting for transfers between devices: 423 us -> none  [the longest x1 158 us: shards(): lax.psum(jnp.dot(attended, output_weight, preferred_element_type=jnp.floa...]
    pallas_call x0 -> x18, Pallas kernels: none -> 237 us  [the longest x4 73.3 us: attend_back(): pl.pallas_call(functools.partial(back_kernel, own, prefix_count, 0), out_...]
    reduce_scatter x5 -> x2, waiting for transfers between devices: 210 us -> 0.01 us  [the longest x1 0.01 us: shards(): lax.psum_scatter(hidden_grad(mid, cotangent, gp, act, batch_size), 'batch...]
    ppermute x0 -> x33, waiting for transfers between devices: none -> 198 us  [the longest x11 133 us: along(): lax.ppermute(values, 'tensor', [(i, i ^ k) for i in range(tensor_size)])]
    dot_general x29 -> x5, matrix products: 112 us -> 3.29 us  [the longest x1 1.56 us: shards(): jnp.einsum('pr,dr->pd', grad_inner, inner_weight.astype(F32), precision=P...]
    ppermute x0 -> x33, starting transfers between devices: none -> 37.7 us  [the longest x22 21.4 us: across(): lax.ppermute(values, 'batch', [(i, i ^ k) for i in range(batch_size)])]
    reduce_sum x11 -> x1, other arithmetic: 34.6 us -> 0.6 us  [shards(): outer_bias_total = jnp.sum(grad_prefix, axis=1)]
    unnamed x123 -> x103, local copies, waits for them, and re-layouts: 15.9 us -> 35.8 us
  transfers between devices with their start and end apart: 8 -> 35, of which waited for: 8 -> 15; matrix products, arithmetic and copies ran while one was open for 7% -> 12% of each run, Pallas kernels for 0% -> 29%
where the time goes in v1:
time: 651 us; the launch traced here: 640 us
  Pallas kernels  237 us (36%)
  waiting for transfers between devices  198 us (30%)
  local copies, waits for them, and re-layouts  78 us (12%)
  blocking collectives  63.1 us (10%)
  starting transfers between devices  37.8 us (6%)
  between operations  15.1 us (2%)
    ppermute x11, waiting for transfers between devices, along(): lax.ppermute(values, 'tensor', [(i, i ^ k) for i in range(tensor_size)])  133 us
    pallas_call x4, Pallas kernels, attend_back(): pl.pallas_call(functools.partial(back_kernel, own, prefix_count, 0), out_...  73.3 us
    ppermute x22, waiting for transfers between devices, across(): lax.ppermute(values, 'batch', [(i, i ^ k) for i in range(batch_size)])  65.3 us
    pallas_call x4, Pallas kernels, attend(): pl.pallas_call(functools.partial(attend_kernel, merge, prefix_count), out...  65 us
    pallas_call x3, Pallas kernels, mix(): pl.pallas_call(functools.partial(mix_kernel, pieces), grid=(length // TB,...  41.8 us
    psum x1, blocking collectives, shards(): grad_hidden_prefix = lax.psum(grad_hidden_part, ('batch', 'tensor'))  37.3 us
    unnamed x103, local copies, waits for them, and re-layouts  35.8 us
    psum x1, blocking collectives, shards(): lax.psum((joint_bias_sum, up_bias_sum, mixed, gain_sums[0:2], gprefix), '...  25.9 us
  transfers between devices with their start and end apart: 35, of which 15 were waited for; matrix products, arithmetic and copies ran while one was open for 12% of the time, Pallas kernels for 29%

profile of v1, /device:TPU:0, one launch (start us, length us, event | category | flops | bytes accessed | tf_op | source)
XLA Modules:
  0.0 640.1 jit_solution(2212910181009228791)
XLA Ops:
  7.3 2.6 hidden_pieces.1
  9.8 3.1 slice_bitcast_fusion
  13.0 3.1 collective-permute-start.28
  16.1 2.6 collective-permute-start.23
  18.6 3.7 head_pieces.1
  22.4 2.3 slice_bitcast_fusion.4
  28.3 56.2 %collective-permute-done.11 = f32[40,256]{1,0:T(8,128)S(1)} collective-permute-done((f32[40,256]{1,0:T(8,128)S(1)}, f32[40,256]{1,0:T(8,128)S(1)}, u32[]{:S(2)}, u32[]{:S(2)}) %collective-permute-start.11) | collective-permute-done | bytes 40992 | tf_op jit(solution)/shard_map/ppermute | solution.py:535
  84.6 2.5 collective-permute-start.18
  87.0 2.5 collective-permute-start.6
  91.0 64.5 %collective-permute-done.6 = f32[128,1024]{1,0:T(8,128)S(1)} collective-permute-done((f32[128,1024]{1,0:T(8,128)}, f32[128,1024]{1,0:T(8,128)S(1)}, u32[]{:S(2)}, u32[]{:S(2)}) %collective-permute-start.6) | collective-permute-done | bytes 524320 | tf_op jit(solution)/shard_map/ppermute | solution.py:535
  162.8 15.3 %attend_own.1 = (bf16[1024,1024]{1,0:T(8,128)(2,1)}, bf16[1024,256]{1,0:T(8,128)(2,1)}, bf16[1024,256]{1,0:T(8,128)(2,1)}, bf16[1024,256]{1,0:T(8,128)(2,1)}, bf...) custom-call(bf16[1024,1024]{1,0:T(8,128)(2,1)} %tok_ref.1, f32[1,1024]{1,0:T(1,128)} %bitcast.131, ...), custom_call_target="tpu_custom_call" | custom-call | tf_op jit(solution)/shard_map/attend_own/pallas_call | solution.py:166
  183.0 1.9 constant_dynamic-update-slice_fusion.10
  184.9 2.4 constant_dynamic-update-slice_fusion.23
  188.5 4.6 collective-permute-done.30
  196.6 2.3 constant_dynamic-update-slice_fusion.15
  198.9 7.1 %collective-permute-done.24 = f32[256,1024]{1,0:T(8,128)} collective-permute-done((f32[256,1024]{1,0:T(8,128)S(1)}, f32[256,1024]{1,0:T(8,128)}, u32[]{:S(2)}, u32[]{:S(2)}) %collective-permute-start.24) | collective-permute-done | bytes 1048608 | tf_op jit(solution)/shard_map/ppermute | solution.py:538
  207.5 8.1 %collective-permute-done.20 = f32[256,1024]{1,0:T(8,128)} collective-permute-done((f32[256,1024]{1,0:T(8,128)}, f32[256,1024]{1,0:T(8,128)}, u32[]{:S(2)}, u32[]{:S(2)}) %collective-permute-start.20) | collective-permute-done | bytes 1048608 | tf_op jit(solution)/shard_map/ppermute | solution.py:538
  217.1 2.3 constant_dynamic-update-slice_fusion.18
  219.4 9.0 %collective-permute-done.19 = f32[256,1024]{1,0:T(8,128)S(1)} collective-permute-done((f32[256,1024]{1,0:T(8,128)}, f32[256,1024]{1,0:T(8,128)S(1)}, u32[]{:S(2)}, u32[]{:S(2)}) %collective-permute-start.19) | collective-permute-done | bytes 1048608 | tf_op jit(solution)/shard_map/ppermute | solution.py:538
  228.3 2.2 collective-permute-start
  231.7 2.4 constant_dynamic-update-slice_fusion.13
  235.1 2.3 constant_dynamic-update-slice_fusion.21
  237.4 4.6 collective-permute-done
  247.6 12.9 %collective-permute-done.26 = f32[256,1024]{1,0:T(8,128)S(1)} collective-permute-done((f32[256,1024]{1,0:T(8,128)}, f32[256,1024]{1,0:T(8,128)S(1)}, u32[]{:S(2)}, u32[]{:S(2)}) %collective-permute-start.26) | collective-permute-done | bytes 1048608 | tf_op jit(solution)/shard_map/ppermute | solution.py:538
  261.5 2.9 collective-permute-done.17
  267.6 4.1 collective-permute-done.8
  274.2 7.8 %collective-permute-done.2 = f32[128,1024]{1,0:T(8,128)S(1)} collective-permute-done((f32[128,1024]{1,0:T(8,128)}, f32[128,1024]{1,0:T(8,128)S(1)}, u32[]{:S(2)}, u32[]{:S(2)}) %collective-permute-start.2) | collective-permute-done | bytes 524320 | tf_op jit(solution)/shard_map/ppermute | solution.py:538
  288.8 6.5 %collective-permute-done.9 = f32[128,1024]{1,0:T(8,128)} collective-permute-done((f32[128,1024]{1,0:T(8,128)}, f32[128,1024]{1,0:T(8,128)}, u32[]{:S(2)}, u32[]{:S(2)}) %collective-permute-start.9) | collective-permute-done | bytes 524320 | tf_op jit(solution)/shard_map/ppermute | solution.py:538
  302.6 5.0 collective-permute-done.3
  308.6 4.7 collective-permute-done.5
  336.4 16.6 %attend_others.3 = (bf16[4,256,1024]{2,1,0:T(8,128)(2,1)}, bf16[1024,256]{1,0:T(8,128)(2,1)}, bf16[1024,256]{1,0:T(8,128)(2,1)}, bf16[1024,256]{1,0:T(8,128)(2,1...) custom-call(bf16[1024,1024]{1,0:T(8,128)(2,1)} %get-tuple-element.72.refs_0_.x_ref, ...), custom_call_target="tpu_custom_call" | custom-call | tf_op jit(solution)/shard_map/attend_others/pallas_call | solution.py:166
  353.0 16.6 %attend_others.4 = (bf16[4,256,1024]{2,1,0:T(8,128)(2,1)}, bf16[1024,256]{1,0:T(8,128)(2,1)}, bf16[1024,256]{1,0:T(8,128)(2,1)}, bf16[1024,256]{1,0:T(8,128)(2,1...) custom-call(bf16[1024,1024]{1,0:T(8,128)(2,1)} %get-tuple-element.72.refs_0_.x_ref, ...), custom_call_target="tpu_custom_call" | custom-call | tf_op jit(solution)/shard_map/attend_others/pallas_call | solution.py:166
  369.5 16.6 %attend_others.5 = (bf16[4,256,1024]{2,1,0:T(8,128)(2,1)}, bf16[1024,256]{1,0:T(8,128)(2,1)}, bf16[1024,256]{1,0:T(8,128)(2,1)}, bf16[1024,256]{1,0:T(8,128)(2,1...) custom-call(bf16[1024,1024]{1,0:T(8,128)(2,1)} %get-tuple-element.72.refs_0_.x_ref, ...), custom_call_target="tpu_custom_call" | custom-call | tf_op jit(solution)/shard_map/attend_others/pallas_call | solution.py:166
  386.1 14.2 %mix_own.1 = (bf16[1024,1024]{1,0:T(8,128)(2,1)}, bf16[1024,1024]{1,0:T(8,128)(2,1)}, bf16[1024,1024]{1,0:T(8,128)(2,1)}, f32[1024,256]{1,0:T(8,128)}, f32[1024,1024]{1,0:T(8,128)}, /*index=5*/f32[1,1024]{1,0:T(1,128)}) custom-call(s32[1]{0:T(128)} %bitcast.z_ref, f32[1024,1024]{1,0:T(8,128)} %get-tuple-element.77.res_ref, bf16[1024,1024]{1,0:T(8,128)(2,1)} %cot_ref.11, ...), custom_call_target="tpu_custom_call" | custom-call | tf_op jit(solution)/shard_map/mix_own/pallas_call | solution.py:292
  400.4 13.9 %mix_others.3 = (f32[1024,256]{1,0:T(8,128)}, f32[1024,1024]{1,0:T(8,128)}) custom-call(s32[1]{0:T(128)} %bitcast.z_ref, bf16[1024,1024]{1,0:T(8,128)(2,1)} %get-tuple-element.78.mid_ref, bf16[1024,1024]{1,0:T(8,128)(2,1)} %cot_ref.11, f32[1024,1024]{1,0:T(8,128)} %constant_dynamic-update-slice_fusion.20.mine_ref, ...), custom_call_target="tpu_custom_call" | custom-call | tf_op jit(solution)/shard_map/mix_others/pallas_call | solution.py:348
  414.3 13.9 %mix_others.4 = (f32[1024,256]{1,0:T(8,128)}, f32[1024,1024]{1,0:T(8,128)}) custom-call(s32[1]{0:T(128)} %bitcast.z_ref, bf16[1024,1024]{1,0:T(8,128)(2,1)} %get-tuple-element.78.mid_ref, bf16[1024,1024]{1,0:T(8,128)(2,1)} %cot_ref.11, f32[1024,1024]{1,0:T(8,128)} %constant_dynamic-update-slice_fusion.16.mine_ref, ...), custom_call_target="tpu_custom_call" | custom-call | tf_op jit(solution)/shard_map/mix_others/pallas_call | solution.py:348
  428.3 13.9 %mix_others.5 = (bf16[1024,256]{1,0:T(8,128)(2,1)}, f32[1024,1024]{1,0:T(8,128)}) custom-call(s32[1]{0:T(128)} %bitcast.z_ref, bf16[1024,1024]{1,0:T(8,128)(2,1)} %get-tuple-element.78.mid_ref, bf16[1024,1024]{1,0:T(8,128)(2,1)} %cot_ref.11, f32[1024,1024]{1,0:T(8,128)} %constant_dynamic-update-slice_fusion.12.mine_ref, ...), custom_call_target="tpu_custom_call" | custom-call | tf_op jit(solution)/shard_map/mix_others/pallas_call | solution.py:348
  442.1 8.5 %residual_back.1 = (bf16[1024,1024]{1,0:T(8,128)(2,1)}, f32[1024,256]{1,0:T(8,128)}, f32[8,1024]{1,0:T(8,128)}) custom-call(s32[1]{0:T(128)} %bitcast.z_ref, f32[1024,1024]{1,0:T(8,128)} %get-tuple-element.77.res_ref, bf16[1024,1024]{1,0:T(8,128)(2,1)} %cot_ref.11, f32[1024,1024]{1,0:T(8,128)} %get-tuple-element.86.gm_ref, f32[1,1024]{1,0:T(1,128)} %bitcast.130), custom_call_target="tpu_custom_call" | custom-call | tf_op jit(solution)/shard_map/residual_back/pallas_call | solution.py:403
  450.6 17.9 %back_own.1 = (bf16[1024,768]{1,0:T(8,128)(2,1)}, f32[2,16,256]{2,1,0:T(8,128)}, f32[1024,1024]{1,0:T(8,128)}) custom-call(bf16[4,256,1024]{2,1,0:T(8,128)(2,1)} %get-tuple-element.71.refs_3_.refs_0_, bf16[1024,256]{1,0:T(8,128)(2,1)} %get-tuple-element.107.refs_1_, bf16[1024,256]{1,0:T(8,128)(2,1)} %get-tuple-element.108.refs_2_, ...), custom_call_target="tpu_custom_call" | custom-call | tf_op jit(solution)/shard_map/back_own/pallas_call | solution.py:249
  468.5 9.5 %head_grad.1 = (f32[8,128,1024]{2,1,0:T(8,128)}, f32[1,768]{1,0:T(1,128)}) custom-call(bf16[1024,1024]{1,0:T(8,128)(2,1)} %get-tuple-element.72.refs_0_.x_ref, bf16[1024,1024]{1,0:T(8,128)(2,1)} %get-tuple-element.94.refs_10_.low_ref, bf16[1024,768]{1,0:T(8,128)(2,1)} %get-tuple-element.115.gj_ref, bf16[256,1024]{1,0:T(8,128)(2,1)} %get-tuple-element.110.refs_4_.att_ref), custom_call_target="tpu_custom_call" | custom-call | tf_op jit(solution)/shard_map/head_grad/pallas_call | solution.py:506
  478.1 12.0 %hidden_grad.1 = f32[8,256,1024]{2,1,0:T(8,128)} custom-call(bf16[1024,1024]{1,0:T(8,128)(2,1)} %get-tuple-element.78.mid_ref, bf16[1024,1024]{1,0:T(8,128)(2,1)} %cot_ref.11, bf16[1024,1024]{1,0:T(8,128)(2,1)} %get-tuple-element.119.gp_ref, bf16[1024,1024]{1,0:T(8,128)(2,1)} %get-tuple-element.120.act_ref), custom_call_target="tpu_custom_call" | custom-call | tf_op jit(solution)/shard_map/hidden_grad/pallas_call | solution.py:479
  490.8 18.3 %back_others.3.refs_11_ = f32[1024,1024]{1,0:T(8,128)} custom-call(bf16[4,256,1024]{2,1,0:T(8,128)(2,1)} %get-tuple-element.101.refs_0_, bf16[1024,256]{1,0:T(8,128)(2,1)} %get-tuple-element.102.refs_1_, bf16[1024,256]{1,0:T(8,128)(2,1)} %get-tuple-element.103.refs_2_, bf16[1024,256]{1,0:T(8,128)(2,1)} %get-tuple-element.104.refs_3_, ...), custom_call_target="tpu_custom_call" | custom-call | tf_op jit(solution)/shard_map/back_others/pallas_call | solution.py:249
  509.0 18.4 %back_others.4.refs_11_ = f32[1024,1024]{1,0:T(8,128)} custom-call(bf16[4,256,1024]{2,1,0:T(8,128)(2,1)} %get-tuple-element.95.refs_0_, bf16[1024,256]{1,0:T(8,128)(2,1)} %get-tuple-element.96.refs_1_, bf16[1024,256]{1,0:T(8,128)(2,1)} %get-tuple-element.97.refs_2_, bf16[1024,256]{1,0:T(8,128)(2,1)} %get-tuple-element.98.refs_3_, ...), custom_call_target="tpu_custom_call" | custom-call | tf_op jit(solution)/shard_map/back_others/pallas_call | solution.py:249
  527.5 18.8 %back_others.5.ga_ref = f32[1024,1024]{1,0:T(8,128)} custom-call(bf16[4,256,1024]{2,1,0:T(8,128)(2,1)} %get-tuple-element.88.refs_0_, bf16[1024,256]{1,0:T(8,128)(2,1)} %get-tuple-element.89.refs_1_, bf16[1024,256]{1,0:T(8,128)(2,1)} %get-tuple-element.90.refs_2_, bf16[1024,256]{1,0:T(8,128)(2,1)} %get-tuple-element.91.refs_3_, ...), custom_call_target="tpu_custom_call" | custom-call | tf_op jit(solution)/shard_map/back_others/pallas_call | solution.py:249
  546.3 6.5 %final_back.1 = (bf16[1024,256]{1,0:T(8,128)(2,1)}, f32[8,256]{1,0:T(8,128)}) custom-call(s32[1]{0:T(128)} %bitcast.z_ref, bf16[1024,1024]{1,0:T(8,128)(2,1)} %tok_ref.1, f32[1024,256]{1,0:T(8,128)} %get-tuple-element.87.part_ref, f32[1024,1024]{1,0:T(8,128)} %back_others.5.ga_ref, f32[1,1024]{1,0:T(1,128)} %bitcast.132), custom_call_target="tpu_custom_call" | custom-call | tf_op jit(solution)/shard_map/final_back/pallas_call | solution.py:447
  553.5 25.9 %all-reduce.1 = (f32[2,256]{1,0:T(2,128)S(1)}, f32[3,256]{1,0:T(4,128)}, f32[4,256]{1,0:T(4,128)S(1)}, f32[1024]{0:T(1024)}, f32[2,10,256]{2,1,0:T(8,128)S(1)}) all-reduce(f32[2,256]{1,0:T(2,128)S(1)} %slice.162, f32[3,256]{1,0:T(4,128)S(1)} %reshape.325, ...), channel_id=1, replica_groups=mesh['batch'=8,'tensor'=4] {'batch'}, use_global_device_ids=true, to_apply=%region_0.1 | all-reduce | flops 8448 | bytes 67584 | tf_op jit(solution)/shard_map/psum | solution.py:607
  581.7 37.3 %psum.46 = f32[10,512]{1,0:T(8,128)S(1)} all-reduce(f32[10,512]{1,0:T(8,128)S(1)} %convolution_bitcast_fusion.1), channel_id=1, replica_groups=mesh['batch'=8,'tensor'=4] {'batch','tensor'}, use_global_device_ids=true, to_apply=%region_6.7 | all-reduce | flops 5120 | bytes 40960 | tf_op jit(solution)/shard_map/psum | solution.py:608
  629.7 2.1 slice_bitcast_fusion.2
  (235 shorter events, 92.8 us)
Async XLA Ops:
  7.2 19.8 %copy-start = (bf16[1024,512]{1,0:T(8,128)(2,1)S(1)}, bf16[1024,512]{1,0:T(8,128)(2,1)}, u32[]{:S(2)}) copy-start(bf16[1024,512]{1,0:T(8,128)(2,1)} %param.35) | copy-start | bytes 3145732
  7.2 618.7 %reduce-scatter.3.cloned.1.call-start = ((), (), s32[]{:S(2)}) async-start(), calls=%async_computation.2 | async-start | bytes 4718592 | tf_op jit(solution)/shard_map/reduce_scatter | solution.py:599
  13.0 144.1 %collective-permute-start.28 = (f32[256,1024]{1,0:T(8,128)}, f32[256,1024]{1,0:T(8,128)}, u32[]{:S(2)}, u32[]{:S(2)}) collective-permute-start(f32[256,1024]{1,0:T(8,128)} %get-tuple-element.186), channel_id=1, source_target_pairs={{0,1},{1,0},{2,3},{3,2},{4,5},{5,4},{6,7},{7,6},{8,9},{9,8},{10,11... | collective-permute-start | bytes 3145736 | tf_op jit(solution)/shard_map/ppermute | solution.py:535
  16.1 143.3 %collective-permute-start.23 = (f32[256,1024]{1,0:T(8,128)}, f32[256,1024]{1,0:T(8,128)S(1)}, u32[]{:S(2)}, u32[]{:S(2)}) collective-permute-start(f32[256,1024]{1,0:T(8,128)} %get-tuple-element.186), channel_id=1, source_target_pairs={{0,2},{1,3},{2,0},{3,1},{4,6},{5,7},{6,4},{7,5},{8,10},{9,11},{10,... | collective-permute-start | bytes 3145736 | tf_op jit(solution)/shard_map/ppermute | solution.py:535
  22.4 138.8 %copy-start.26 = (s32[1,1024]{1,0:T(1,128)S(1)}, s32[1,1024]{1,0:T(1,128)}, u32[]{:S(2)}) copy-start(s32[1,1024]{1,0:T(1,128)} %refs_9_.7) | copy-start | bytes 12292
  24.7 62.3 %collective-permute-start.12 = (f32[128,1024]{1,0:T(8,128)}, f32[128,1024]{1,0:T(8,128)}, u32[]{:S(2)}, u32[]{:S(2)}) collective-permute-start(f32[128,1024]{1,0:T(8,128)} %get-tuple-element.190), channel_id=1, source_target_pairs={{0,1},{1,0},{2,3},{3,2},{4,5},{5,4},{6,7},{7,6},{8,9},{9,8},{10,11... | collective-permute-start | bytes 1572872 | tf_op jit(solution)/shard_map/ppermute | solution.py:535
  25.2 64.3 %collective-permute-start.15 = (f32[128,1024]{1,0:T(8,128)}, f32[128,1024]{1,0:T(8,128)S(1)}, u32[]{:S(2)}, u32[]{:S(2)}) collective-permute-start(f32[128,1024]{1,0:T(8,128)} %get-tuple-element.189), channel_id=1, source_target_pairs={{0,1},{1,0},{2,3},{3,2},{4,5},{5,4},{6,7},{7,6},{8,9},{9,8},{10,11... | collective-permute-start | bytes 1572872 | tf_op jit(solution)/shard_map/ppermute | solution.py:535
  28.0 150.1 %copy-start.30 = (f32[40,256]{1,0:T(8,128)}, f32[40,256]{1,0:T(8,128)S(1)}, u32[]{:S(2)}) copy-start(f32[40,256]{1,0:T(8,128)S(1)} %maximum_maximum_fusion) | copy-start | bytes 122884
  28.0 56.6 %collective-permute-start.11 = (f32[40,256]{1,0:T(8,128)S(1)}, f32[40,256]{1,0:T(8,128)S(1)}, u32[]{:S(2)}, u32[]{:S(2)}) collective-permute-start(f32[40,256]{1,0:T(8,128)S(1)} %maximum_maximum_fusion), channel_id=1, source_target_pairs={{0,2},{1,3},{2,0},{3,1},{4,6},{5,7},{6,4},{7,5},{8,10},{9,11},{10,... | collective-permute-start | bytes 122888 | tf_op jit(solution)/shard_map/ppermute | solution.py:535
  84.6 75.4 %collective-permute-start.18 = (f32[256,1024]{1,0:T(8,128)}, f32[256,1024]{1,0:T(8,128)}, u32[]{:S(2)}, u32[]{:S(2)}) collective-permute-start(f32[256,1024]{1,0:T(8,128)} %get-tuple-element.186), channel_id=1, source_target_pairs={{0,3},{1,2},{2,1},{3,0},{4,7},{5,6},{6,5},{7,4},{8,11},{9,10},{10,... | collective-permute-start | bytes 3145736 | tf_op jit(solution)/shard_map/ppermute | solution.py:535
  87.0 68.5 %collective-permute-start.6 = (f32[128,1024]{1,0:T(8,128)}, f32[128,1024]{1,0:T(8,128)S(1)}, u32[]{:S(2)}, u32[]{:S(2)}) collective-permute-start(f32[128,1024]{1,0:T(8,128)} %get-tuple-element.190), channel_id=1, source_target_pairs={{0,2},{1,3},{2,0},{3,1},{4,6},{5,7},{6,4},{7,5},{8,10},{9,11},{10,... | collective-permute-start | bytes 1572872 | tf_op jit(solution)/shard_map/ppermute | solution.py:535
  89.5 67.5 %copy-start.18 = (f32[128,1024]{1,0:T(8,128)}, f32[128,1024]{1,0:T(8,128)S(1)}, u32[]{:S(2)}) copy-start(f32[128,1024]{1,0:T(8,128)S(1)} %collective-permute-done.15) | copy-start | bytes 1572868
  89.5 69.1 %collective-permute-start.13 = (f32[128,1024]{1,0:T(8,128)}, f32[128,1024]{1,0:T(8,128)S(1)}, u32[]{:S(2)}, u32[]{:S(2)}) collective-permute-start(f32[128,1024]{1,0:T(8,128)} %collective-permute-done.12), channel_id=1, source_target_pairs={{0,8},{4,12},{8,0},{12,4},{16,24},{20,28},{24,16},{28,20},{1,9},{5... | collective-permute-start | bytes 1572872 | tf_op jit(solution)/shard_map/ppermute | solution.py:538
  155.5 24.0 %collective-permute-start.14 = (f32[128,1024]{1,0:T(8,128)}, f32[128,1024]{1,0:T(8,128)}, u32[]{:S(2)}, u32[]{:S(2)}) collective-permute-start(f32[128,1024]{1,0:T(8,128)} %collective-permute-done.12), channel_id=1, source_target_pairs={{0,16},{4,20},{8,24},{12,28},{16,0},{20,4},{24,8},{28,12},{1,17},{... | collective-permute-start | bytes 1572872 | tf_op jit(solution)/shard_map/ppermute | solution.py:538
  157.1 31.3 %collective-permute-start.29 = (f32[256,1024]{1,0:T(8,128)}, f32[256,1024]{1,0:T(8,128)S(1)}, u32[]{:S(2)}, u32[]{:S(2)}) collective-permute-start(f32[256,1024]{1,0:T(8,128)} %collective-permute-done.28), channel_id=1, source_target_pairs={{0,8},{4,12},{8,0},{12,4},{16,24},{20,28},{24,16},{28,20},{1,9},{5... | collective-permute-start | bytes 3145736 | tf_op jit(solution)/shard_map/ppermute | solution.py:538
  158.6 34.5 %collective-permute-start.30 = (f32[256,1024]{1,0:T(8,128)}, f32[256,1024]{1,0:T(8,128)}, u32[]{:S(2)}, u32[]{:S(2)}) collective-permute-start(f32[256,1024]{1,0:T(8,128)} %collective-permute-done.28), channel_id=1, source_target_pairs={{0,16},{4,20},{8,24},{12,28},{16,0},{20,4},{24,8},{28,12},{1,17},{... | collective-permute-start | bytes 3145736 | tf_op jit(solution)/shard_map/ppermute | solution.py:538
  159.4 46.6 %collective-permute-start.24 = (f32[256,1024]{1,0:T(8,128)S(1)}, f32[256,1024]{1,0:T(8,128)}, u32[]{:S(2)}, u32[]{:S(2)}) collective-permute-start(f32[256,1024]{1,0:T(8,128)S(1)} %collective-permute-done.23), channel_id=1, source_target_pairs={{0,8},{4,12},{8,0},{12,4},{16,24},{20,28},{24,16},{28,20},{1,9},{5... | collective-permute-start | bytes 3145736 | tf_op jit(solution)/shard_map/ppermute | solution.py:538
  160.0 55.6 %collective-permute-start.20 = (f32[256,1024]{1,0:T(8,128)}, f32[256,1024]{1,0:T(8,128)}, u32[]{:S(2)}, u32[]{:S(2)}) collective-permute-start(f32[256,1024]{1,0:T(8,128)} %collective-permute-done.18), channel_id=1, source_target_pairs={{0,16},{4,20},{8,24},{12,28},{16,0},{20,4},{24,8},{28,12},{1,17},{... | collective-permute-start | bytes 3145736 | tf_op jit(solution)/shard_map/ppermute | solution.py:538
  179.5 48.8 %collective-permute-start.19 = (f32[256,1024]{1,0:T(8,128)}, f32[256,1024]{1,0:T(8,128)S(1)}, u32[]{:S(2)}, u32[]{:S(2)}) collective-permute-start(f32[256,1024]{1,0:T(8,128)} %collective-permute-done.18), channel_id=1, source_target_pairs={{0,8},{4,12},{8,0},{12,4},{16,24},{20,28},{24,16},{28,20},{1,9},{5... | collective-permute-start | bytes 3145736 | tf_op jit(solution)/shard_map/ppermute | solution.py:538
  188.4 18.3 %copy-start.19 = (f32[128,1024]{1,0:T(8,128)S(1)}, f32[128,1024]{1,0:T(8,128)}, u32[]{:S(2)}) copy-start(f32[128,1024]{1,0:T(8,128)} %copy-done.18) | copy-start | bytes 1572868
  188.4 55.1 %collective-permute-start.31 = (f32[256,1024]{1,0:T(8,128)S(1)}, f32[256,1024]{1,0:T(8,128)S(1)}, u32[]{:S(2)}, u32[]{:S(2)}) collective-permute-start(f32[256,1024]{1,0:T(8,128)S(1)} %copy-done.8), channel_id=1, source_target_pairs={{0,1},{1,0},{2,3},{3,2},{4,5},{5,4},{6,7},{7,6},{8,9},{9,8},{10,11... | collective-permute-start | bytes 3145736 | tf_op jit(solution)/shard_map/ppermute | solution.py:535
  193.1 51.7 %collective-permute-start.25 = (f32[256,1024]{1,0:T(8,128)S(1)}, f32[256,1024]{1,0:T(8,128)S(1)}, u32[]{:S(2)}, u32[]{:S(2)}) collective-permute-start(f32[256,1024]{1,0:T(8,128)S(1)} %collective-permute-done.23), channel_id=1, source_target_pairs={{0,16},{4,20},{8,24},{12,28},{16,0},{20,4},{24,8},{28,12},{1,17},{... | collective-permute-start | bytes 3145736 | tf_op jit(solution)/shard_map/ppermute | solution.py:538
  206.0 54.4 %collective-permute-start.26 = (f32[256,1024]{1,0:T(8,128)}, f32[256,1024]{1,0:T(8,128)S(1)}, u32[]{:S(2)}, u32[]{:S(2)}) collective-permute-start(f32[256,1024]{1,0:T(8,128)} %collective-permute-done.24), channel_id=1, source_target_pairs={{0,16},{4,20},{8,24},{12,28},{16,0},{20,4},{24,8},{28,12},{1,17},{... | collective-permute-start | bytes 3145736 | tf_op jit(solution)/shard_map/ppermute | solution.py:538
  215.6 50.4 %collective-permute-start.21 = (f32[256,1024]{1,0:T(8,128)}, f32[256,1024]{1,0:T(8,128)S(1)}, u32[]{:S(2)}, u32[]{:S(2)}) collective-permute-start(f32[256,1024]{1,0:T(8,128)} %collective-permute-done.20), channel_id=1, source_target_pairs={{0,8},{4,12},{8,0},{12,4},{16,24},{20,28},{24,16},{28,20},{1,9},{5... | collective-permute-start | bytes 3145736 | tf_op jit(solution)/shard_map/ppermute | solution.py:538
  228.3 13.6 %collective-permute-start = (f32[128,1024]{1,0:T(8,128)}, f32[128,1024]{1,0:T(8,128)}, u32[]{:S(2)}, u32[]{:S(2)}) collective-permute-start(f32[128,1024]{1,0:T(8,128)} %get-tuple-element.190), channel_id=1, source_target_pairs={{0,3},{1,2},{2,1},{3,0},{4,7},{5,6},{6,5},{7,4},{8,11},{9,10},{10,... | collective-permute-start | bytes 1572872 | tf_op jit(solution)/shard_map/ppermute | solution.py:535
  237.4 23.0 %copy-start.31 = (f32[40,256]{1,0:T(8,128)S(1)}, f32[40,256]{1,0:T(8,128)}, u32[]{:S(2)}) copy-start(f32[40,256]{1,0:T(8,128)} %copy-done.30) | copy-start | bytes 122884
  242.0 25.1 %collective-permute-start.7 = (f32[128,1024]{1,0:T(8,128)S(1)}, f32[128,1024]{1,0:T(8,128)}, u32[]{:S(2)}, u32[]{:S(2)}) collective-permute-start(f32[128,1024]{1,0:T(8,128)S(1)} %copy-done.16), channel_id=1, source_target_pairs={{0,8},{4,12},{8,0},{12,4},{16,24},{20,28},{24,16},{28,20},{1,9},{5... | collective-permute-start | bytes 1572872 | tf_op jit(solution)/shard_map/ppermute | solution.py:538
  243.5 28.2 %collective-permute-start.8 = (f32[128,1024]{1,0:T(8,128)S(1)}, f32[128,1024]{1,0:T(8,128)S(1)}, u32[]{:S(2)}, u32[]{:S(2)}) collective-permute-start(f32[128,1024]{1,0:T(8,128)S(1)} %copy-done.16), channel_id=1, source_target_pairs={{0,16},{4,20},{8,24},{12,28},{16,0},{20,4},{24,8},{28,12},{1,17},{... | collective-permute-start | bytes 1572872 | tf_op jit(solution)/shard_map/ppermute | solution.py:538
  244.8 27.2 %collective-permute-start.1 = (f32[128,1024]{1,0:T(8,128)}, f32[128,1024]{1,0:T(8,128)S(1)}, u32[]{:S(2)}, u32[]{:S(2)}) collective-permute-start(f32[128,1024]{1,0:T(8,128)} %collective-permute-done), channel_id=1, source_target_pairs={{0,8},{4,12},{8,0},{12,4},{16,24},{20,28},{24,16},{28,20},{1,9},{5... | collective-permute-start | bytes 1572872 | tf_op jit(solution)/shard_map/ppermute | solution.py:538
  260.4 4.0 collective-permute-start.17
  264.4 17.5 %collective-permute-start.2 = (f32[128,1024]{1,0:T(8,128)}, f32[128,1024]{1,0:T(8,128)S(1)}, u32[]{:S(2)}, u32[]{:S(2)}) collective-permute-start(f32[128,1024]{1,0:T(8,128)} %collective-permute-done), channel_id=1, source_target_pairs={{0,16},{4,20},{8,24},{12,28},{16,0},{20,4},{24,8},{28,12},{1,17},{... | collective-permute-start | bytes 1572872 | tf_op jit(solution)/shard_map/ppermute | solution.py:538
  265.9 47.4 %collective-permute-start.16 = (f32[512,1024]{1,0:T(8,128)}, f32[512,1024]{1,0:T(8,128)}, u32[]{:S(2)}, u32[]{:S(2)}) collective-permute-start(f32[512,1024]{1,0:T(8,128)} %constant_dynamic-update-slice_fusion.8.refs_1_), channel_id=1, source_target_pairs={{0,4},{4,0},{8,12},{12,8},{16,20},{20,16},{24,28},{28,24},{1,5},{5... | collective-permute-start | bytes 6291464 | tf_op jit(solution)/shard_map/ppermute | solution.py:538
  267.1 133.3 %collective-permute-start.32 = (f32[1024,1024]{1,0:T(8,128)}, f32[1024,1024]{1,0:T(8,128)}, u32[]{:S(2)}, u32[]{:S(2)}) collective-permute-start(f32[1024,1024]{1,0:T(8,128)} %constant_dynamic-update-slice_fusion.20.mine_ref), channel_id=1, source_target_pairs={{0,4},{4,0},{8,12},{12,8},{16,20},{20,16},{24,28},{28,24},{1,5},{5... | collective-permute-start | bytes 12582920 | tf_op jit(solution)/shard_map/ppermute | solution.py:538
  271.6 142.7 %collective-permute-start.27 = (f32[1024,1024]{1,0:T(8,128)}, f32[1024,1024]{1,0:T(8,128)}, u32[]{:S(2)}, u32[]{:S(2)}) collective-permute-start(f32[1024,1024]{1,0:T(8,128)} %constant_dynamic-update-slice_fusion.16.mine_ref), channel_id=1, source_target_pairs={{0,4},{4,0},{8,12},{12,8},{16,20},{20,16},{24,28},{28,24},{1,5},{5... | collective-permute-start | bytes 12582920 | tf_op jit(solution)/shard_map/ppermute | solution.py:538
  272.0 156.2 %collective-permute-start.22 = (f32[1024,1024]{1,0:T(8,128)}, f32[1024,1024]{1,0:T(8,128)}, u32[]{:S(2)}, u32[]{:S(2)}) collective-permute-start(f32[1024,1024]{1,0:T(8,128)} %constant_dynamic-update-slice_fusion.12.mine_ref), channel_id=1, source_target_pairs={{0,4},{4,0},{8,12},{12,8},{16,20},{20,16},{24,28},{28,24},{1,5},{5... | collective-permute-start | bytes 12582920 | tf_op jit(solution)/shard_map/ppermute | solution.py:538
  281.9 13.3 %collective-permute-start.9 = (f32[128,1024]{1,0:T(8,128)}, f32[128,1024]{1,0:T(8,128)}, u32[]{:S(2)}, u32[]{:S(2)}) collective-permute-start(f32[128,1024]{1,0:T(8,128)} %collective-permute-done.7), channel_id=1, source_target_pairs={{0,16},{4,20},{8,24},{12,28},{16,0},{20,4},{24,8},{28,12},{1,17},{... | collective-permute-start | bytes 1572872 | tf_op jit(solution)/shard_map/ppermute | solution.py:538
  295.3 12.3 %collective-permute-start.3 = (f32[128,1024]{1,0:T(8,128)}, f32[128,1024]{1,0:T(8,128)S(1)}, u32[]{:S(2)}, u32[]{:S(2)}) collective-permute-start(f32[128,1024]{1,0:T(8,128)} %copy-done.23), channel_id=1, source_target_pairs={{0,8},{4,12},{8,0},{12,4},{16,24},{20,28},{24,16},{28,20},{1,9},{5... | collective-permute-start | bytes 1572872 | tf_op jit(solution)/shard_map/ppermute | solution.py:538
  299.7 14.1 %copy-start.5 = (f32[40,2,2,2,32]{4,3,2,1,0:T(2,128)S(1)}, f32[40,2,2,2,32]{4,3,2,1,0:T(2,128)}, u32[]{:S(2)}) copy-start(f32[40,2,2,2,32]{4,3,2,1,0:T(2,128)} %copy-done.4) | copy-start | bytes 122884
  299.7 14.1 %copy-start.7 = (f32[40,2,2,2,32]{4,3,2,1,0:T(2,128)S(1)}, f32[40,2,2,2,32]{4,3,2,1,0:T(2,128)}, u32[]{:S(2)}) copy-start(f32[40,2,2,2,32]{4,3,2,1,0:T(2,128)} %copy-done.6) | copy-start | bytes 122884
  299.8 14.1 %copy-start.9 = (f32[40,1,2,4,32]{4,3,2,0,1:T(4,128)S(1)}, f32[40,1,2,4,32]{4,3,2,0,1:T(4,128)}, u32[]{:S(2)}) copy-start(f32[40,1,2,4,32]{4,3,2,0,1:T(4,128)} %rev.32) | copy-start | bytes 122884
  299.8 14.1 %copy-start.10 = (f32[40,1,2,4,32]{4,3,2,0,1:T(4,128)S(1)}, f32[40,1,2,4,32]{4,3,2,0,1:T(4,128)}, u32[]{:S(2)}) copy-start(f32[40,1,2,4,32]{4,3,2,0,1:T(4,128)} %rev.35) | copy-start | bytes 122884
  307.6 5.8 collective-permute-start.5
  308.6 15.9 %copy-start.1 = (f32[512,1024]{1,0:T(8,128)}, f32[512,1024]{1,0:T(8,128)S(1)}, u32[]{:S(2)}) copy-start(f32[512,1024]{1,0:T(8,128)S(1)} %constant_dynamic-update-slice_fusion.refs_1_) | copy-start | bytes 6291460
  313.4 39.6 %collective-permute-start.10 = (f32[512,1024]{1,0:T(8,128)}, f32[512,1024]{1,0:T(8,128)}, u32[]{:S(2)}, u32[]{:S(2)}) collective-permute-start(f32[512,1024]{1,0:T(8,128)} %constant_dynamic-update-slice_fusion.4.refs_1_), channel_id=1, source_target_pairs={{0,4},{4,0},{8,12},{12,8},{16,20},{20,16},{24,28},{28,24},{1,5},{5... | collective-permute-start | bytes 6291464 | tf_op jit(solution)/shard_map/ppermute | solution.py:538
  313.4 56.2 %collective-permute-start.4 = (f32[512,1024]{1,0:T(8,128)S(1)}, f32[512,1024]{1,0:T(8,128)}, u32[]{:S(2)}, u32[]{:S(2)}) collective-permute-start(f32[512,1024]{1,0:T(8,128)S(1)} %constant_dynamic-update-slice_fusion.refs_1_), channel_id=1, source_target_pairs={{0,4},{4,0},{8,12},{12,8},{16,20},{20,16},{24,28},{28,24},{1,5},{5... | collective-permute-start | bytes 6291464 | tf_op jit(solution)/shard_map/ppermute | solution.py:538
  478.0 151.7 %reduce-scatter.5.cloned.1.call-start = ((), (), s32[]{:S(2)}) async-start(), calls=%async_computation.3 | async-start | bytes 9437184 | tf_op jit(solution)/shard_map/reduce_scatter | solution.py:590
  546.3 34.9 %copy-start.3 = (bf16[512,2,256]{2,1,0:T(2,128)(2,1)S(1)}, bf16[512,2,256]{2,1,0:T(2,128)(2,1)}, u32[]{:S(2)}) copy-start(bf16[512,2,256]{2,1,0:T(2,128)(2,1)} %param.37) | copy-start | bytes 1572868
  546.3 72.7 %copy-start.28 = (f32[10,1024]{1,0:T(8,128)S(1)}, f32[10,1024]{1,0:T(8,128)}, u32[]{:S(2)}) copy-start(f32[10,1024]{1,0:T(8,128)} %param.34) | copy-start | bytes 122884
  (27 other events, 192.7 us)
Sparse Core Ops, SparseCore 0:
  478.2 50.1 reduce-scatter.2
  532.2 72.4 reduce-scatter.4

commit v2 on v1

--- a/solution.py
+++ b/solution.py
@@ -105,10 +105,33 @@
     return jnp.where(allowed, 0.0, NEGATIVE)
 
 
-def attend_kernel(merge, prefix_count, *refs):
+def reorder(values, member, dim=1):
+    block = values.shape[dim] // 8
+    place = lax.broadcasted_iota(jnp.int32, values.shape, dim) // block
+    for bit in (1, 2, 4):
+        up = pltpu.roll(values, block * bit, dim)
+        down = pltpu.roll(values, values.shape[dim] - block * bit, dim)
+        turned = jnp.where((place & bit) != 0, up, down)
+        values = jnp.where((member & bit) != 0, turned, values)
+    return values
+
+
+def column_of(seg_row):
+    wide = jnp.broadcast_to(seg_row.astype(F32), (128, seg_row.shape[1]))
+    return wide.T[:, 0:1].astype(jnp.int32)
+
+
+def extras(member_ref, small_ref, merge):
+    small = small_ref[0:40, :]
     if merge:
-        x_ref, mine_ref, theirs_ref, bias_ref, pk_ref, pv_ref, segc_ref, segr_ref, acc_ref = refs[:9]
-        w_ref, q_ref, k_ref, v_ref, att_ref, lse_ref, out_ref, mask_ref, vt_ref = refs[9:]
+        small = reorder(small, member_ref[0])
+    return small[0:PAD].astype(BF16), small[PAD : 2 * PAD].astype(BF16), small[2 * PAD : 2 * PAD + 8]
+
+
+def attend_kernel(merge, prefix_count, member_ref, *refs):
+    if merge:
+        x_ref, mine_ref, theirs_ref, small_ref, segr_ref, acc_ref = refs[:6]
+        w_ref, q_ref, k_ref, v_ref, att_ref, lse_ref, out_ref, mask_ref, vt_ref = refs[6:]
         half = HD // 2
         for g in range(GROUP):
             for c in range(4):
@@ -116,24 +139,25 @@
                 w_ref[c, g * HD : g * HD + half, :] = mine_ref[piece, :].astype(BF16)
                 w_ref[c, g * HD + half : (g + 1) * HD, :] = theirs_ref[piece, :].astype(BF16)
     else:
-        tok_ref, gain_ref, shift_ref, w_ref, bias_ref, pk_ref, pv_ref, segc_ref, segr_ref, acc_ref = refs[:10]
-        x_ref, q_ref, k_ref, v_ref, att_ref, lse_ref, out_ref, mask_ref, vt_ref = refs[10:]
+        tok_ref, gain_ref, shift_ref, w_ref, small_ref, segr_ref, acc_ref = refs[:7]
+        x_ref, q_ref, k_ref, v_ref, att_ref, lse_ref, out_ref, mask_ref, vt_ref = refs[7:]
         for t in range(0, tok_ref.shape[0], TB):
             normed, _ = normalize(tok_ref[t : t + TB, :].astype(F32))
             x_ref[t : t + TB, :] = (normed * gain_ref[...] + shift_ref[...]).astype(BF16)
+    pk, pv, bias = extras(member_ref, small_ref, merge)
+    seg_col = column_of(segr_ref[...])
     length = x_ref.shape[0]
     x = x_ref[...]
-    q_ref[...] = ((dot(x, w_ref[0], NT) + bias_ref[0:1, :]) * HD ** (-0.5)).astype(BF16)
-    k_ref[...] = (dot(x, w_ref[1], NT) + bias_ref[1:2, :]).astype(BF16)
-    v_ref[...] = (dot(x, w_ref[2], NT) + bias_ref[2:3, :]).astype(BF16)
+    q_ref[...] = ((dot(x, w_ref[0], NT) + bias[0:1]) * HD ** (-0.5)).astype(BF16)
+    k_ref[...] = (dot(x, w_ref[1], NT) + bias[1:2]).astype(BF16)
+    v_ref[...] = (dot(x, w_ref[2], NT) + bias[2:3]).astype(BF16)
     vt_ref[...] = v_ref[...].T
-    pvt = pv_ref[...].astype(BF16).T
-    pk = pk_ref[...].astype(BF16)
+    pvt = pv.T
     live = lax.broadcasted_iota(jnp.int32, (PAD, QB), 0) < prefix_count
     heads = head_of_lane(QB)
     for i in range(length // QB):
         first, last, rows = first_key(i, length), (i + 1) * QB, slice(i * QB, (i + 1) * QB)
-        mask_ref[first:last, :] = mask_tile(segc_ref[first:last, :], segr_ref[:, rows], first, last, i * QB)
+        mask_ref[first:last, :] = mask_tile(seg_col[first:last], segr_ref[:, rows], first, last, i * QB)
         for h in range(GROUP):
             span = slice(h * HD, (h + 1) * HD)
             asked = jnp.where(heads == h, q_ref[rows, :], jnp.zeros((), BF16))
@@ -161,28 +185,31 @@
     ]
 
 
-def attend(merge, prefix_count, length, width, args):
+def attend(merge, prefix_count, length, width, *args):
     first = shape_of((4, WIDE, width), BF16) if merge else shape_of((length, width), BF16)
+    vm = pl.BlockSpec(memory_space=pltpu.VMEM)
     return pl.pallas_call(
         functools.partial(attend_kernel, merge, prefix_count),
         out_shape=[first] + attend_outs(length, width),
+        in_specs=[pl.BlockSpec(memory_space=pltpu.SMEM)] + [vm] * (len(args) - 1),
         scratch_shapes=[pltpu.VMEM((length, QB), F32), pltpu.VMEM((WIDE, length), BF16)],
         compiler_params=params(),
         name="attend_others" if merge else "attend_own",
     )(*args)
 
 
-def back_kernel(own, prefix_count, own_start, *refs):
-    w_ref, q_ref, k_ref, v_ref, att_ref, lse_ref, pk_ref, pv_ref, segc_ref, segr_ref, gr_ref = refs[:11]
+def back_kernel(own, prefix_count, member_ref, *refs):
+    w_ref, q_ref, k_ref, v_ref, att_ref, lse_ref, small_ref, segr_ref, gr_ref = refs[:9]
     if own:
-        gj_ref, gp_ref, out_ref, mask_ref, kt_ref, p_ref, ds_ref, do_ref, dot_ref, dqt_ref, dk_ref, dv_ref, qm_ref, gm_ref = refs[11:]
+        gj_ref, gp_ref, out_ref, mask_ref, kt_ref, p_ref, ds_ref, do_ref, dot_ref, dqt_ref, dk_ref, dv_ref, qm_ref, gm_ref = refs[9:]
     else:
-        acc_ref, out_ref, mask_ref, kt_ref, p_ref, ds_ref, do_ref, dot_ref, dqt_ref, dk_ref, dv_ref, qm_ref, gm_ref, gj_ref = refs[11:]
+        acc_ref, out_ref, mask_ref, kt_ref, p_ref, ds_ref, do_ref, dot_ref, dqt_ref, dk_ref, dv_ref, qm_ref, gm_ref, gj_ref = refs[9:]
     length = q_ref.shape[0]
     do_ref[...] = dot(gr_ref[...], w_ref[3], NT).astype(BF16)
     dot_ref[...] = do_ref[...].T
     kt_ref[...] = k_ref[...].T
-    pk, pv = pk_ref[...].astype(BF16), pv_ref[...].astype(BF16)
+    pk, pv, _ = extras(member_ref, small_ref, not own)
+    seg_col = column_of(segr_ref[...])
     pkt = pk.T
     live = lax.broadcasted_iota(jnp.int32, (PAD, QB), 0) < prefix_count
     heads = head_of_lane(QB)
@@ -193,7 +220,7 @@
     gpv = jnp.zeros((PAD, WIDE), F32)
     for i in range(length // QB):
         first, last, rows = first_key(i, length), (i + 1) * QB, slice(i * QB, (i + 1) * QB)
-        mask_ref[first:last, :] = mask_tile(segc_ref[first:last, :], segr_ref[:, rows], first, last, i * QB)
+        mask_ref[first:last, :] = mask_tile(seg_col[first:last], segr_ref[:, rows], first, last, i * QB)
         for h in range(GROUP):
             span, lanes = slice(h * HD, (h + 1) * HD), slice(h * QB, (h + 1) * QB)
             asked = jnp.where(heads == h, q_ref[rows, :], zero)
@@ -226,8 +253,8 @@
         out_ref[...] = acc_ref[...] + part
 
 
-def attend_back(own, prefix_count, args):
-    length, width = args[10].shape
+def attend_back(own, prefix_count, *args):
+    length, width = args[9].shape
     outs = [shape_of((length, width), F32)]
     scratch = [
         pltpu.VMEM((length, QB), F32),
@@ -247,8 +274,9 @@
     else:
         scratch = scratch + [pltpu.VMEM((length, 3 * WIDE), BF16)]
     return pl.pallas_call(
-        functools.partial(back_kernel, own, prefix_count, 0),
+        functools.partial(back_kernel, own, prefix_count),
         out_shape=outs,
+        in_specs=[pl.BlockSpec(memory_space=pltpu.SMEM)] + [pl.BlockSpec(memory_space=pltpu.VMEM)] * (len(args) - 1),
         scratch_shapes=scratch,
         compiler_params=params(),
         name="back_own" if own else "back_others",
@@ -284,7 +312,7 @@
     bsum_ref[...] += jnp.sum(gp.astype(F32), axis=0, keepdims=True)
 
 
-def mix_own(z, residual, cotangent, gain, shift, up, up_bias, down, down_bias, own_width):
+def mix_own(own_width, z, residual, cotangent, gain, shift, up, up_bias, down, down_bias):
     length, width = residual.shape
     hidden = up.shape[1]
     rows = lambda w: pl.BlockSpec((TB, w), lambda t: (t, 0))
@@ -317,7 +345,7 @@
     )(z, residual, cotangent, gain, shift, up, up_bias, down, down_bias)
 
 
-def mix_kernel(pieces, z_ref, mid_ref, cot_ref, mine_ref, theirs_ref, bias_ref, share_in, gm_in, share_ref, gm_ref, up_ref, down_ref, part_ref):
+def mix_kernel(pieces, begin, z_ref, mid_ref, cot_ref, mine_ref, theirs_ref, small_ref, share_in, gm_in, share_ref, gm_ref, up_ref, down_ref, part_ref):
     rows = mine_ref.shape[0] // pieces // 2
     start = pl.multiple_of(z_ref[0] * share_ref.shape[1], share_ref.shape[1])
     own = pl.ds(start, share_ref.shape[1])
@@ -332,21 +360,23 @@
         part_ref[...] = down_ref[:, own]
 
     mid = mid_ref[...]
-    act, slope = gelu_pair(dot(mid, up_ref[...], NT) + bias_ref[...])
+    biases = reorder(small_ref[40:48, 0:rows], z_ref[1], 0)
+    bias = jnp.concatenate([biases[2 * begin + j : 2 * begin + j + 1] for j in range(2 * pieces)], axis=1)
+    act, slope = gelu_pair(dot(mid, up_ref[...], NT) + bias)
     gp = (dot(cot_ref[...], down_ref[...], NT) * slope).astype(BF16)
     share_ref[...] = (share_in[...] + dot(act.astype(BF16), part_ref[...])).astype(share_ref.dtype)
     gm_ref[...] = gm_in[...] + dot(gp, up_ref[...])
 
 
-def mix(z, mid, cotangent, mine, theirs, bias, share, gm, last):
+def mix(z, mid, cotangent, mine, theirs, bias, share, gm, begin, last):
     length, width = mid.shape
-    pieces = 4
+    pieces = mine.shape[0] // 256
     hidden = mine.shape[0]
     own_width = share.shape[1]
     rows = lambda w: pl.BlockSpec((TB, w), lambda t: (t, 0))
     whole = lambda a: pl.BlockSpec(a.shape, lambda t: (0, 0), pipeline_mode=pl.Buffered(1))
     return pl.pallas_call(
-        functools.partial(mix_kernel, pieces),
+        functools.partial(mix_kernel, pieces, begin),
         grid=(length // TB,),
         in_specs=[
             pl.BlockSpec(memory_space=pltpu.SMEM),
@@ -469,7 +499,7 @@
             out_ref[a, at : at + per, :] = grad[a * per : (a + 1) * per]
 
 
-def hidden_grad(mid, cotangent, gp, act, parts):
+def hidden_grad(parts, mid, cotangent, gp, act):
     length, width = mid.shape
     hidden = gp.shape[1]
     rows = 128
@@ -526,7 +556,7 @@
     batch_size, tensor_size = lax.axis_size("batch"), lax.axis_size("tensor")
     z = lax.axis_index("tensor").astype(jnp.int32)
     member = (lax.axis_index("batch") % 8).astype(jnp.int32)
-    z_arr, member_arr = z.reshape(1), member.reshape(1)
+    member_arr, places = member.reshape(1), jnp.stack([z, member])
 
     def own_columns(values):
         return lax.dynamic_slice_in_dim(values, z * local, local, values.ndim - 1)
@@ -537,76 +567,180 @@
     def across(values, k):
         return lax.ppermute(values, "batch", [(i, i ^ k) for i in range(batch_size)])
 
+    now = [member_arr]
+
+    def after(values):
+        return lax.optimization_barrier((values, *now))[0]
+
+    def wait(*values):
+        held = lax.optimization_barrier((*values, *now))
+        now[:] = [held[0]]
+        return held[0] if len(values) == 1 else held[: len(values)]
+
+    def run(call, *args):
+        held = lax.optimization_barrier((*args, *now))
+        outs = call(*held[: len(args)])
+        now[:] = [outs[-1] if isinstance(outs, (list, tuple)) else outs]
+        return outs
+
     row = lambda v: v.reshape(1, -1)
-    own_heads, send_heads = head_pieces(member_arr, joint_weight, output_weight)
-    send_hidden = hidden_pieces(member_arr, up_weight, down_weight)
-
-    hidden_prefix = jnp.tanh(jnp.dot(prefix_table, inner_weight.astype(F32), precision=PRECISE) + inner_bias)
-    outer_float = outer_weight.astype(F32)
-    prefix_pairs = jnp.einsum("pr,rke->kpe", hidden_prefix, outer_float, precision=PRECISE) + outer_bias[:, None, :]
-    prefix_padded = jnp.pad(prefix_pairs, ((0, 0), (0, PAD - prefix_count), (0, 0)))
-
-    small = jnp.concatenate([prefix_padded.reshape(2 * PAD, local), joint_bias, up_bias.reshape(8, hidden // 256, 32).transpose(1, 0, 2).reshape(-1, local), jnp.zeros((1, local), F32)], axis=0)
-
-    def reorder(values):
-        parts = values.reshape(values.shape[0], 8, local // 8)
-        for bit in (1, 2, 4):
-            turned = parts.reshape(values.shape[0], 4 // bit, 2, bit, local // 8)[:, :, ::-1].reshape(parts.shape)
-            parts = jnp.where((member & bit) > 0, turned, parts)
-        return parts.reshape(values.shape)
-
-    smalls = [reorder(along(small, k)) for k in (1, 2, 3)]
-
-    def plane(first, diagonal, turn):
-        x1, y1 = across(first, 2), across(first, 4)
-        if diagonal is None:
-            diagonal = across(x1, 4) if turn == 2 else across(y1, 2)
-        mine = jnp.concatenate([first, x1, y1, diagonal], axis=0)
-        return mine, across(mine, 1)
-
-    def slots(send):
-        return [
-            plane(along(send[0], 1), along(send[1], 1), 1),
-            plane(along(send[0], 2), None, 2),
-            plane(along(send[0], 3), None, 3),
-        ]
-
-    seg_row = segment_ids
-    seg_col = segment_ids.reshape(length, 1)
-    others = slots(send_heads)
-    x, *saved, residual = attend(
-        False, prefix_count, length, width,
-        (tokens, row(attention_gain), row(attention_shift), own_heads, joint_bias, prefix_padded[0], prefix_padded[1], seg_col, seg_row, row(output_bias)),
-    )
-    groups = [(own_heads, saved, prefix_padded[0], prefix_padded[1])]
-    for (mine, theirs), extra in zip(others, smalls):
-        pk, pv, bias = extra[0:PAD], extra[PAD : 2 * PAD], extra[2 * PAD : 2 * PAD + 3]
-        w, *saved, residual = attend(True, prefix_count, length, width, (x, mine, theirs, bias, pk, pv, seg_col, seg_row, residual))
-        groups.append((w, saved, pk, pv))
-
-    mid, act, gp, share, gm, up_bias_sum = mix_own(
-        z_arr, residual, cotangent, row(mixer_gain), row(mixer_shift), up_weight, row(up_bias), down_weight, row(down_bias), local
-    )
-    hidden_sum = lax.psum_scatter(hidden_grad(mid, cotangent, gp, act, batch_size), "batch", scatter_dimension=0, tiled=False)
-    for k, ((mine, theirs), extra) in enumerate(zip(slots(send_hidden), smalls)):
-        bias = extra[2 * PAD + 3 : 2 * PAD + 3 + hidden // 256].reshape(hidden // 256, 8, 32).transpose(1, 0, 2).reshape(1, hidden)
-        share, gm = mix(z_arr, mid, cotangent, mine, theirs, bias, share, gm, k == 2)
-    low, part, sums = residual_back(z_arr, residual, cotangent, gm, row(mixer_gain), local)
-
-    w, saved, pk, pv = groups[0]
-    gj, gprefix, ga = attend_back(True, prefix_count, (w, *saved, pk, pv, seg_col, seg_row, low))
-    head_parts, joint_bias_sum = head_grad(x, low, gj, saved[3])
-    head_sum = lax.psum_scatter(head_parts.reshape(batch_size, -1, 3 * local + local), "batch", scatter_dimension=0, tiled=False)
-    gprefix = gprefix[:, :prefix_count]
-    grad_hidden_part = jnp.einsum("kpe,rke->pr", gprefix, outer_float, precision=PRECISE)
-    for w, saved, pk, pv in groups[1:]:
-        (ga,) = attend_back(False, prefix_count, (w, *saved, pk, pv, seg_col, seg_row, low, ga))
-    tokens_gradient, gain_sums = final_back(z_arr, tokens, part, ga, row(attention_gain))
-
-    mixed = own_columns(sums[0:4])
-    totals = lax.psum((joint_bias_sum, up_bias_sum, mixed, gain_sums[0:2], gprefix), "batch")
-    grad_hidden_prefix = lax.psum(grad_hidden_part, ("batch", "tensor"))
-    joint_bias_total, up_bias_total, mixed_total, gain_total, grad_prefix = totals
+    stack = lambda *parts: jnp.concatenate(parts, axis=0)
+
+    own_heads, send_heads = run(head_pieces, member_arr, joint_weight, output_weight)
+    a1 = along(after(send_heads[0]), 1)
+    send_hidden = run(hidden_pieces, member_arr, up_weight, down_weight)
+    a2 = along(after(send_heads[0]), 2)
+
+    def prefixes(prefix_table, inner_weight):
+        hidden_prefix = jnp.tanh(jnp.dot(prefix_table, inner_weight.astype(F32), precision=PRECISE) + inner_bias)
+        pairs = jnp.einsum("pr,rke->kpe", hidden_prefix, outer_weight.astype(F32), precision=PRECISE)
+        pairs = jnp.pad(pairs + outer_bias[:, None, :], ((0, 0), (0, PAD - prefix_count), (0, 0)))
+        ups = jnp.pad(up_bias.reshape(8, hidden // 8), ((0, 0), (0, local - hidden // 8)))
+        joints = jnp.pad(joint_bias, ((0, 5), (0, 0)))
+        return hidden_prefix, stack(pairs.reshape(2 * PAD, local), joints, ups)
+
+    hidden_prefix, small = run(prefixes, prefix_table, inner_weight)
+    smalls = [along(after(small), k) for k in (1, 2, 3)]
+    a1 = wait(a1)
+    a1x, a1y = across(after(a1), 2), across(after(a1), 4)
+    x, *saved, residual = run(
+        functools.partial(attend, False, prefix_count, length, width),
+        member_arr, tokens, row(attention_gain), row(attention_shift), own_heads, small, segment_ids, row(output_bias),
+    )
+    groups = [(own_heads, saved, small)]
+
+    def attend_more(mine, theirs, extra, residual):
+        w, *saved, residual = run(
+            functools.partial(attend, True, prefix_count, length, width),
+            member_arr, x, mine, theirs, extra, segment_ids, residual,
+        )
+        groups.append((w, saved, extra))
+        return residual
+
+    a1x, a1y, a2, *smalls = wait(a1x, a1y, a2, *smalls)
+    a1d, a3 = along(after(send_heads[1]), 1), along(after(send_heads[0]), 3)
+    a2x, a2y = across(after(a2), 2), across(after(a2), 4)
+    a1d = wait(a1d)
+    mine = run(stack, a1, a1x, a1y, a1d)
+    theirs = across(after(mine), 1)
+    theirs = wait(theirs)
+    f1 = along(after(send_hidden[0]), 1)
+    residual = attend_more(mine, theirs, smalls[0], residual)
+
+    a2x, a2y, a3 = wait(a2x, a2y, a3)
+    a2d = across(after(a2x), 4)
+    a3x, a3y = across(after(a3), 2), across(after(a3), 4)
+    f2 = along(after(send_hidden[0]), 2)
+    a2d = wait(a2d)
+    mine = run(stack, a2, a2x, a2y, a2d)
+    theirs = across(after(mine), 1)
+    theirs = wait(theirs)
+    residual = attend_more(mine, theirs, smalls[1], residual)
+
+    a3x, a3y, f1 = wait(a3x, a3y, f1)
+    a3d = across(after(a3y), 2)
+    f1x, f1y = across(after(f1), 2), across(after(f1), 4)
+    a3d = wait(a3d)
+    mine = run(stack, a3, a3x, a3y, a3d)
+    theirs = across(after(mine), 1)
+    theirs = wait(theirs)
+    f1d = along(after(send_hidden[1]), 1)
+    residual = attend_more(mine, theirs, smalls[2], residual)
+
+    mid, act, gp, share, gm, up_bias_sum = run(
+        functools.partial(mix_own, local),
+        places, residual, cotangent, row(mixer_gain), row(mixer_shift), up_weight, row(up_bias), down_weight,
+        row(down_bias),
+    )
+    f1x, f1y, f2 = wait(f1x, f1y, f2)
+    f2x, f2y = across(after(f2), 2), across(after(f2), 4)
+    f3 = along(after(send_hidden[0]), 3)
+    f1d = wait(f1d)
+    mine = run(stack, f1, f1x, f1y, f1d)
+    theirs = across(after(mine), 1)
+    hidden_part = run(functools.partial(hidden_grad, batch_size), mid, cotangent, gp, act)
+    theirs = wait(theirs)
+
+    def mix_more(mine, theirs, extra, share, gm, begin, last):
+        return run(
+            functools.partial(mix, begin=begin, last=last), places, mid, cotangent, mine, theirs, extra, share, gm
+        )
+
+    share, gm = mix_more(mine, theirs, smalls[0], share, gm, 0, False)
+    f2x, f2y, f3 = wait(f2x, f2y, f3)
+    f2d = across(after(f2x), 4)
+    f3x, f3y = across(after(f3), 2), across(after(f3), 4)
+    f2d = wait(f2d)
+    mine = run(stack, f2, f2x, f2y, f2d)
+    theirs = across(after(mine), 1)
+    theirs = wait(theirs)
+    share, gm = mix_more(mine, theirs, smalls[1], share, gm, 0, False)
+    f3x, f3y = wait(f3x, f3y)
+    cut = f3.shape[0] // 2
+    f3d = [across(after(f3x[:cut]), 4), across(after(f3y[cut:]), 2)]
+    mine = run(stack, f3, f3x, f3y)
+    theirs = across(after(mine), 1)
+    theirs = wait(theirs)
+    share, gm = mix_more(mine, theirs, smalls[2], share, gm, 0, False)
+    f3d = wait(*f3d)
+    mine = run(stack, *f3d)
+    theirs = across(after(mine), 1)
+    theirs = wait(theirs)
+    share, gm = mix_more(mine, theirs, smalls[2], share, gm, 3, True)
+    hidden_sum = lax.psum_scatter(after(hidden_part), "batch", scatter_dimension=0, tiled=False)
+
+    low, part, sums = run(
+        functools.partial(residual_back, own_width=local), places, residual, cotangent, gm, row(mixer_gain)
+    )
+    w, saved, extra = groups[0]
+    gj, gprefix, ga = run(
+        functools.partial(attend_back, True, prefix_count), member_arr, w, *saved, extra, segment_ids, low
+    )
+    head_part, joint_bias_sum = run(head_grad, x, low, gj, saved[3])
+    head_sum = lax.psum_scatter(
+        after(head_part.reshape(batch_size, -1, 4 * local)), "batch", scatter_dimension=0, tiled=False
+    )
+
+    def sums_before(gprefix, sums, joint_bias_sum, up_bias_sum):
+        part = jnp.einsum("kpe,rke->pr", gprefix[:, :prefix_count], outer_weight.astype(F32), precision=PRECISE)
+        rows = [gprefix.reshape(2 * PAD, local), own_columns(sums[0:4]), joint_bias_sum.reshape(3, local)]
+        rows += [jnp.zeros((1, local), F32), up_bias_sum.reshape(-1, local), part.reshape(-1, local)]
+        return stack(*rows)
+
+    totals = run(sums_before, gprefix, sums, joint_bias_sum, up_bias_sum)
+    turns = [1 << b for b in range((batch_size - 1).bit_length())]
+    more = [(across, k) for k in turns] + [(along, 1 << b) for b in range((tensor_size - 1).bit_length())]
+    split = 2 * PAD + 8 + hidden // local
+    batch_totals = None
+    for g, (w, saved, extra) in enumerate(groups[1:]):
+        pending = None
+        if more:
+            send, k = more.pop(0)
+            pending = send(after(totals), k)
+        (ga,) = run(
+            functools.partial(attend_back, False, prefix_count), member_arr, w, *saved, extra, segment_ids, low, ga
+        )
+        if pending is not None:
+            totals = run(jnp.add, totals, wait(pending))
+            if g + 1 == len(turns):
+                batch_totals = totals
+    while len(more) > tensor_size.bit_length() - 1:
+        send, k = more.pop(0)
+        totals = run(jnp.add, totals, wait(send(after(totals), k)))
+        batch_totals = totals
+    pending = more[0][0](after(totals), more[0][1])
+    tokens_gradient, gain_sums = run(final_back, places, tokens, part, ga, row(attention_gain))
+    totals = run(jnp.add, totals, wait(pending))
+    for send, k in more[1:]:
+        totals = run(jnp.add, totals, wait(send(after(totals), k)))
+    for k in turns:
+        gain_sums = run(jnp.add, gain_sums, wait(across(after(gain_sums), k)))
+
+    grad_prefix = batch_totals[: 2 * PAD].reshape(2, PAD, local)[:, :prefix_count]
+    mixed_total = batch_totals[2 * PAD : 2 * PAD + 4]
+    joint_bias_total = batch_totals[2 * PAD + 4 : 2 * PAD + 7]
+    up_bias_total = batch_totals[2 * PAD + 8 : split]
+    grad_hidden_prefix = totals[split:].reshape(prefix_count, -1)
     outer_rows = outer_weight.shape[0] // batch_size
     hidden_own = lax.dynamic_slice_in_dim(hidden_prefix, lax.axis_index("batch") * outer_rows, outer_rows, 1)
     outer_total = jnp.einsum("pr,kpe->rke", hidden_own, grad_prefix, precision=PRECISE)
@@ -624,10 +758,10 @@
     return (
         share,
         tokens_gradient,
-        gain_total[0],
-        gain_total[1],
+        gain_sums[0],
+        gain_sums[1],
         joint_total,
-        joint_bias_total.reshape(3, local),
+        joint_bias_total,
         output_total,
         mixed_total[2],
         mixed_total[0],

time: 651 us -> 533 us (0.82)
  blocking collectives: 63.1 us -> 0 us
  local copies, waits for them, and re-layouts: 78 us -> 39.8 us
  waiting for transfers between devices: 198 us -> 162 us
  starting transfers between devices: 37.8 us -> 54.7 us
    ppermute x11 -> x13, waiting for transfers between devices: 133 us -> 55.9 us  [along(): lax.ppermute(values, 'tensor', [(i, i ^ k) for i in range(tensor_size)])]
    psum x2 -> x0, blocking collectives: 63.1 us -> none  [the longest x1 37.3 us: shards(): grad_hidden_prefix = lax.psum(grad_hidden_part, ('batch', 'tensor'))]
    reduce_scatter x2, waiting for transfers between devices: 0.01 us -> 34 us  [the longest x1 34 us: shards(): lax.psum_scatter(after(hidden_part), 'batch', scatter_dimension=0, tiled=...]
    ppermute x11 -> x13, starting transfers between devices: 16.3 us -> 38.5 us  [along(): lax.ppermute(values, 'tensor', [(i, i ^ k) for i in range(tensor_size)])]
    unnamed x103 -> x97, local copies, waits for them, and re-layouts: 35.8 us -> 26.8 us
    slice x18 -> x7, local copies, waits for them, and re-layouts: 8.98 us -> 1.27 us  [the longest x1 0.59 us: shards(): joint_bias_total = batch_totals[2 * PAD + 4:2 * PAD + 7]]
    reshape x16 -> x4, local copies, waits for them, and re-layouts: 7.09 us -> 0.04 us  [the longest x1 0.02 us: sums_before(): part.reshape(-1, local)]
    pallas_call x7 -> x8, Pallas kernels: 115 us -> 122 us  [the longest x4 73.3 us: attend_back(): pl.pallas_call(functools.partial(back_kernel, own, prefix_count), out_sha...]
  transfers between devices with their start and end apart: 35 -> 45, of which waited for: 15 -> 19; matrix products, arithmetic and copies ran while one was open for 12% -> 4% of each run, Pallas kernels for 29% -> 37%
where the time goes in v2:
time: 533 us; the launch traced here: 523 us
  Pallas kernels  243 us (46%)
  waiting for transfers between devices  162 us (30%)
  starting transfers between devices  54.7 us (10%)
  local copies, waits for them, and re-layouts  39.8 us (7%)
  between operations  15.2 us (3%)
    pallas_call x4, Pallas kernels, attend_back(): pl.pallas_call(functools.partial(back_kernel, own, prefix_count), out_sha...  73.3 us
    ppermute x30, waiting for transfers between devices, across(): lax.ppermute(values, 'batch', [(i, i ^ k) for i in range(batch_size)])  71.8 us
    pallas_call x4, Pallas kernels, attend(): pl.pallas_call(functools.partial(attend_kernel, merge, prefix_count), out...  64.2 us
    ppermute x13, waiting for transfers between devices, along(): lax.ppermute(values, 'tensor', [(i, i ^ k) for i in range(tensor_size)])  55.9 us
    pallas_call x4, Pallas kernels, mix(): pl.pallas_call(functools.partial(mix_kernel, pieces, begin), grid=(length...  48.6 us
    ppermute x13, starting transfers between devices, along(): lax.ppermute(values, 'tensor', [(i, i ^ k) for i in range(tensor_size)])  38.5 us
    reduce_scatter x1, waiting for transfers between devices, shards(): lax.psum_scatter(after(hidden_part), 'batch', scatter_dimension=0, tiled=...  34 us
    unnamed x97, local copies, waits for them, and re-layouts  26.8 us
  transfers between devices with their start and end apart: 45, of which 19 were waited for; matrix products, arithmetic and copies ran while one was open for 4% of the time, Pallas kernels for 37%

profile of v2, /device:TPU:0, one launch (start us, length us, event | category | flops | bytes accessed | tf_op | source)
XLA Modules:
  0.0 522.8 jit_solution(287920939722417053)
XLA Ops:
  7.3 3.7 head_pieces.1
  12.4 3.1 collective-permute-start
  15.5 2.5 hidden_pieces.1
  17.9 2.6 collective-permute-start.3
  21.5 14.6 %collective-permute-done = f32[128,1024]{1,0:T(8,128)S(1)} collective-permute-done((f32[128,1024]{1,0:T(8,128)S(1)}, f32[128,1024]{1,0:T(8,128)S(1)}, u32[]{:S(2)}, u32[]{:S(2)}) %collective-permute-start) | collective-permute-done | bytes 524320 | tf_op jit(solution)/shard_map/ppermute | solution.py:565
  39.2 3.0 collective-permute-start.5
  42.3 3.2 collective-permute-done.4.refs_3_.small_ref.refs_6_
  45.4 2.7 collective-permute-start.6
  48.1 15.1 %attend_own.1 = (bf16[1024,1024]{1,0:T(8,128)(2,1)}, bf16[1024,256]{1,0:T(8,128)(2,1)}, bf16[1024,256]{1,0:T(8,128)(2,1)}, bf16[1024,256]{1,0:T(8,128)(2,1)}, bf...) custom-call(s32[1]{0:T(128)} %bitcast.1.member_ref, bf16[1024,1024]{1,0:T(8,128)(2,1)} %tok_ref, ...), custom_call_target="tpu_custom_call" | custom-call | tf_op jit(solution)/shard_map/attend_own/pallas_call | solution.py:191
  63.4 13.4 %collective-permute-done.10 = f32[128,1024]{1,0:T(8,128)S(1)} collective-permute-done((f32[128,1024]{1,0:T(8,128)S(1)}, f32[128,1024]{1,0:T(8,128)S(1)}, u32[]{:S(2)}, u32[]{:S(2)}) %collective-permute-start.10) | collective-permute-done | bytes 524320 | tf_op jit(solution)/shard_map/ppermute | solution.py:565
  77.4 3.8 collective-permute-done.11.refs_2_
  82.5 16.4 %attend_others.3 = (bf16[4,256,1024]{2,1,0:T(8,128)(2,1)}, bf16[1024,256]{1,0:T(8,128)(2,1)}, bf16[1024,256]{1,0:T(8,128)(2,1)}, bf16[1024,256]{1,0:T(8,128)(2,1...) custom-call(s32[1]{0:T(128)} %bitcast.1.member_ref, ...), custom_call_target="tpu_custom_call" | custom-call | tf_op jit(solution)/shard_map/attend_others/pallas_call | solution.py:191
  99.0 13.9 %collective-permute-done.15 = f32[128,1024]{1,0:T(8,128)S(1)} collective-permute-done((f32[128,1024]{1,0:T(8,128)S(1)}, f32[128,1024]{1,0:T(8,128)S(1)}, u32[]{:S(2)}, u32[]{:S(2)}) %collective-permute-start.15) | collective-permute-done | bytes 524320 | tf_op jit(solution)/shard_map/ppermute | solution.py:568
  115.2 3.5 collective-permute-start.14
  120.4 16.4 %attend_others.4 = (bf16[4,256,1024]{2,1,0:T(8,128)(2,1)}, bf16[1024,256]{1,0:T(8,128)(2,1)}, bf16[1024,256]{1,0:T(8,128)(2,1)}, bf16[1024,256]{1,0:T(8,128)(2,1...) custom-call(s32[1]{0:T(128)} %bitcast.1.member_ref, ...), custom_call_target="tpu_custom_call" | custom-call | tf_op jit(solution)/shard_map/attend_others/pallas_call | solution.py:191
  136.8 5.5 %collective-permute-done.14 = f32[256,1024]{1,0:T(8,128)} collective-permute-done((f32[256,1024]{1,0:T(8,128)}, f32[256,1024]{1,0:T(8,128)}, u32[]{:S(2)}, u32[]{:S(2)}) %collective-permute-start.14) | collective-permute-done | bytes 1048608 | tf_op jit(solution)/shard_map/ppermute | solution.py:565
  142.4 13.2 %collective-permute-done.17 = f32[128,1024]{1,0:T(8,128)S(1)} collective-permute-done((f32[128,1024]{1,0:T(8,128)S(1)}, f32[128,1024]{1,0:T(8,128)S(1)}, u32[]{:S(2)}, u32[]{:S(2)}) %collective-permute-start.17) | collective-permute-done | bytes 524320 | tf_op jit(solution)/shard_map/ppermute | solution.py:568
  157.8 2.2 collective-permute-done.18.refs_2_
  163.4 16.3 %attend_others.5 = (bf16[4,256,1024]{2,1,0:T(8,128)(2,1)}, bf16[1024,256]{1,0:T(8,128)(2,1)}, bf16[1024,256]{1,0:T(8,128)(2,1)}, bf16[1024,256]{1,0:T(8,128)(2,1...) custom-call(s32[1]{0:T(128)} %bitcast.1.member_ref, ...), custom_call_target="tpu_custom_call" | custom-call | tf_op jit(solution)/shard_map/attend_others/pallas_call | solution.py:191
  179.7 14.6 %mix_own.1 = (bf16[1024,1024]{1,0:T(8,128)(2,1)}, bf16[1024,1024]{1,0:T(8,128)(2,1)}, bf16[1024,1024]{1,0:T(8,128)(2,1)}, f32[1024,256]{1,0:T(8,128)}, f32[1024,1024]{1,0:T(8,128)}, /*index=5*/f32[1,1024]{1,0:T(1,128)}) custom-call(s32[2]{0:T(128)} %pad_add_fusion.z_ref, f32[1024,1024]{1,0:T(8,128)} %get-tuple-element.528.res_ref, ...), custom_call_target="tpu_custom_call" | custom-call | tf_op jit(solution)/shard_map/mix_own/pallas_call | solution.py:320
  194.3 11.0 %collective-permute-done.21 = f32[256,1024]{1,0:T(8,128)} collective-permute-done((f32[256,1024]{1,0:T(8,128)}, f32[256,1024]{1,0:T(8,128)}, u32[]{:S(2)}, u32[]{:S(2)}) %collective-permute-start.21) | collective-permute-done | bytes 1048608 | tf_op jit(solution)/shard_map/ppermute | solution.py:565
  205.3 3.2 collective-permute-done.25
  208.4 2.3 constant_dynamic-update-slice_fusion.15
  210.7 2.3 constant_dynamic-update-slice_fusion.14
  213.1 2.3 constant_dynamic-update-slice_fusion.13
  215.4 2.4 constant_dynamic-update-slice_fusion.12.mine_ref
  221.0 11.6 %hidden_grad.1 = f32[8,256,1024]{2,1,0:T(8,128)} custom-call(bf16[1024,1024]{1,0:T(8,128)(2,1)} %get-tuple-element.518.mid_ref, bf16[1024,1024]{1,0:T(8,128)(2,1)} %cot_ref.6, bf16[1024,1024]{1,0:T(8,128)(2,1)} %get-tuple-element.455.gp_ref, bf16[1024,1024]{1,0:T(8,128)(2,1)} %get-tuple-element.456.act_ref), custom_call_target="tpu_custom_call" | custom-call | tf_op jit(solution)/shard_map/hidden_grad/pallas_call | solution.py:509
  232.6 13.9 %mix_others.4 = (f32[1024,256]{1,0:T(8,128)}, f32[1024,1024]{1,0:T(8,128)}) custom-call(s32[2]{0:T(128)} %pad_add_fusion.z_ref, bf16[1024,1024]{1,0:T(8,128)(2,1)} %get-tuple-element.518.mid_ref, bf16[1024,1024]{1,0:T(8,128)(2,1)} %cot_ref.6, f32[1024,1024]{1,0:T(8,128)} %constant_dynamic-update-slice_fusion.12.mine_ref, ...), custom_call_target="tpu_custom_call" | custom-call | tf_op jit(solution)/shard_map/mix_others/pallas_call | solution.py:378
  247.9 23.5 %collective-permute-done.29 = f32[256,1024]{1,0:T(8,128)S(1)} collective-permute-done((f32[256,1024]{1,0:T(8,128)S(1)}, f32[256,1024]{1,0:T(8,128)S(1)}, u32[]{:S(2)}, u32[]{:S(2)}) %collective-permute-start.29) | collective-permute-done | bytes 1048608 | tf_op jit(solution)/shard_map/ppermute | solution.py:568
  275.8 4.9 collective-permute-done.30.theirs_ref
  280.7 2.1 copy-done.4
  282.8 13.9 %mix_others.5 = (f32[1024,256]{1,0:T(8,128)}, f32[1024,1024]{1,0:T(8,128)}) custom-call(s32[2]{0:T(128)} %pad_add_fusion.z_ref, bf16[1024,1024]{1,0:T(8,128)(2,1)} %get-tuple-element.518.mid_ref, bf16[1024,1024]{1,0:T(8,128)(2,1)} %cot_ref.6, f32[1024,1024]{1,0:T(8,128)} %copy-done.2, f32[1024,1024]{1,0:T(8,128)} %copy-done.4, f32[48,256]{1,0:T(8,128)} %copy-done.24, ...), custom_call_target="tpu_custom_call" | custom-call | tf_op jit(solution)/shard_map/mix_others/pallas_call | solution.py:378
  296.7 2.6 collective-permute-done.27
  303.3 3.5 collective-permute-done.33.theirs_ref
  308.5 12.0 %mix_others.6 = (f32[1024,256]{1,0:T(8,128)}, f32[1024,1024]{1,0:T(8,128)}) custom-call(s32[2]{0:T(128)} %pad_add_fusion.z_ref, bf16[1024,1024]{1,0:T(8,128)(2,1)} %get-tuple-element.518.mid_ref, bf16[1024,1024]{1,0:T(8,128)(2,1)} %cot_ref.6, f32[768,1024]{1,0:T(8,128)} %copy-done.3, f32[768,1024]{1,0:T(8,128)} %copy-done.8, f32[48,256]{1,0:T(8,128)} %copy-done.20, ...), custom_call_target="tpu_custom_call" | custom-call | tf_op jit(solution)/shard_map/mix_others/pallas_call | solution.py:378
  320.8 2.5 collective-permute-done.34.theirs_ref
  324.4 8.8 %mix_others.7 = (bf16[1024,256]{1,0:T(8,128)(2,1)}, f32[1024,1024]{1,0:T(8,128)}) custom-call(s32[2]{0:T(128)} %pad_add_fusion.z_ref, bf16[1024,1024]{1,0:T(8,128)(2,1)} %get-tuple-element.518.mid_ref, bf16[1024,1024]{1,0:T(8,128)(2,1)} %cot_ref.6, f32[256,1024]{1,0:T(8,128)} %copy-done.9, f32[256,1024]{1,0:T(8,128)} %copy-done.15, f32[48,256]{1,0:T(8,128)} %copy-done.20, ...), custom_call_target="tpu_custom_call" | custom-call | tf_op jit(solution)/shard_map/mix_others/pallas_call | solution.py:378
  333.2 8.1 %residual_back.1 = (bf16[1024,1024]{1,0:T(8,128)(2,1)}, f32[1024,256]{1,0:T(8,128)}, f32[8,1024]{1,0:T(8,128)}) custom-call(s32[2]{0:T(128)} %pad_add_fusion.z_ref, f32[1024,1024]{1,0:T(8,128)} %get-tuple-element.528.res_ref, bf16[1024,1024]{1,0:T(8,128)(2,1)} %cot_ref.6, f32[1024,1024]{1,0:T(8,128)} %get-tuple-element.530.gm_ref, f32[1,1024]{1,0:T(1,128)} %bitcast.66), custom_call_target="tpu_custom_call" | custom-call | tf_op jit(solution)/shard_map/residual_back/pallas_call | solution.py:433
  341.2 17.7 %back_own.1 = (bf16[1024,768]{1,0:T(8,128)(2,1)}, f32[2,16,256]{2,1,0:T(8,128)}, f32[1024,1024]{1,0:T(8,128)}) custom-call(s32[1]{0:T(128)} %bitcast.1.member_ref, bf16[4,256,1024]{2,1,0:T(8,128)(2,1)} %get-tuple-element.559.refs_3_.refs_0_, bf16[1024,256]{1,0:T(8,128)(2,1)} %get-tuple-element.560.refs_1_, bf16[1024,256]{1,0:T(8,128)(2,1)} %get-tuple-element.561.refs_2_, ...), custom_call_target="tpu_custom_call" | custom-call | tf_op jit(solution)/shard_map/back_own/pallas_call | solution.py:276
  358.9 9.5 %head_grad.1 = (f32[8,128,1024]{2,1,0:T(8,128)}, f32[1,768]{1,0:T(1,128)}) custom-call(bf16[1024,1024]{1,0:T(8,128)(2,1)} %get-tuple-element.571.refs_0_.x_ref, bf16[1024,1024]{1,0:T(8,128)(2,1)} %get-tuple-element.619.refs_8_.low_ref, bf16[1024,768]{1,0:T(8,128)(2,1)} %get-tuple-element.573.gj_ref, bf16[256,1024]{1,0:T(8,128)(2,1)} %get-tuple-element.574.refs_4_.att_ref), custom_call_target="tpu_custom_call" | custom-call | tf_op jit(solution)/shard_map/head_grad/pallas_call | solution.py:536
  372.1 18.0 %back_others.3.refs_9_ = f32[1024,1024]{1,0:T(8,128)} custom-call(s32[1]{0:T(128)} %bitcast.1.member_ref, bf16[4,256,1024]{2,1,0:T(8,128)(2,1)} %get-tuple-element.581.refs_0_, bf16[1024,256]{1,0:T(8,128)(2,1)} %get-tuple-element.582.refs_1_, bf16[1024,256]{1,0:T(8,128)(2,1)} %get-tuple-element.583.refs_2_, bf16[1024,256]{1,0:T(8,128)(2,1)} %get-tuple-element.584.refs_3_, ...), custom_call_target="tpu_custom_call" | custom-call | tf_op jit(solution)/shard_map/back_others/pallas_call | solution.py:276
  391.8 19.2 %back_others.4.refs_9_ = f32[1024,1024]{1,0:T(8,128)} custom-call(s32[1]{0:T(128)} %bitcast.1.member_ref, bf16[4,256,1024]{2,1,0:T(8,128)(2,1)} %get-tuple-element.596.refs_0_, bf16[1024,256]{1,0:T(8,128)(2,1)} %get-tuple-element.597.refs_1_, bf16[1024,256]{1,0:T(8,128)(2,1)} %get-tuple-element.598.refs_2_, bf16[1024,256]{1,0:T(8,128)(2,1)} %get-tuple-element.599.refs_3_, ...), custom_call_target="tpu_custom_call" | custom-call | tf_op jit(solution)/shard_map/back_others/pallas_call | solution.py:276
  411.5 18.4 %back_others.5.ga_ref = f32[1024,1024]{1,0:T(8,128)} custom-call(s32[1]{0:T(128)} %bitcast.1.member_ref, bf16[4,256,1024]{2,1,0:T(8,128)(2,1)} %get-tuple-element.611.refs_0_, bf16[1024,256]{1,0:T(8,128)(2,1)} %get-tuple-element.612.refs_1_, bf16[1024,256]{1,0:T(8,128)(2,1)} %get-tuple-element.613.refs_2_, bf16[1024,256]{1,0:T(8,128)(2,1)} %get-tuple-element.614.refs_3_, ...), custom_call_target="tpu_custom_call" | custom-call | tf_op jit(solution)/shard_map/back_others/pallas_call | solution.py:276
  429.9 18.9 %collective-permute-start.38 = (f32[64,256]{1,0:T(8,128)S(1)}, f32[64,256]{1,0:T(8,128)S(1)}, u32[]{:S(2)}, u32[]{:S(2)}) collective-permute-start(f32[64,256]{1,0:T(8,128)S(1)} %add.72), channel_id=1, source_target_pairs={{0,1},{1,0},{2,3},{3,2},{4,5},{5,4},{6,7},{7,6},{8,9},{9,8},{10,11... | collective-permute-start | bytes 196616 | tf_op jit(solution)/shard_map/ppermute | solution.py:565
  451.7 7.0 %final_back.1 = (bf16[1024,256]{1,0:T(8,128)(2,1)}, f32[8,256]{1,0:T(8,128)}) custom-call(s32[2]{0:T(128)} %pad_add_fusion.z_ref, bf16[1024,1024]{1,0:T(8,128)(2,1)} %tok_ref, f32[1024,256]{1,0:T(8,128)} %get-tuple-element.627.part_ref, f32[1024,1024]{1,0:T(8,128)} %back_others.5.ga_ref, f32[1,1024]{1,0:T(1,128)} %bitcast.68), custom_call_target="tpu_custom_call" | custom-call | tf_op jit(solution)/shard_map/final_back/pallas_call | solution.py:477
  459.4 5.1 collective-permute-done.39
  478.7 34.0 %reduce-scatter.5.cloned.1.call-done = f32[1,256,1024]{2,1,0:T(8,128)} async-done(((f32[8,256,1024]{2,1,0:T(8,128)}), f32[1,256,1024]{2,1,0:T(8,128)}) %reduce-scatter.5.cloned.1.call-update) | async-done | bytes 1048592 | tf_op jit(solution)/shard_map/reduce_scatter | solution.py:690
  512.7 2.1 slice_bitcast_fusion.2
  (210 shorter events, 57.1 us)
Async XLA Ops:
  7.2 467.7 %reduce-scatter.3.cloned.1.call-start = ((), (), s32[]{:S(2)}) async-start(), calls=%async_computation.2 | async-start | bytes 4718592 | tf_op jit(solution)/shard_map/reduce_scatter | solution.py:700
  12.4 23.7 %collective-permute-start = (f32[128,1024]{1,0:T(8,128)S(1)}, f32[128,1024]{1,0:T(8,128)S(1)}, u32[]{:S(2)}, u32[]{:S(2)}) collective-permute-start(f32[128,1024]{1,0:T(8,128)S(1)} %get-tuple-element.365), channel_id=1, source_target_pairs={{0,1},{1,0},{2,3},{3,2},{4,5},{5,4},{6,7},{7,6},{8,9},{9,8},{10,11... | collective-permute-start | bytes 1572872 | tf_op jit(solution)/shard_map/ppermute | solution.py:565
  17.9 45.3 %collective-permute-start.3 = (f32[128,1024]{1,0:T(8,128)S(1)}, f32[128,1024]{1,0:T(8,128)S(1)}, u32[]{:S(2)}, u32[]{:S(2)}) collective-permute-start(f32[128,1024]{1,0:T(8,128)S(1)} %get-tuple-element.365), channel_id=1, source_target_pairs={{0,2},{1,3},{2,0},{3,1},{4,6},{5,7},{6,4},{7,5},{8,10},{9,11},{10,... | collective-permute-start | bytes 1572872 | tf_op jit(solution)/shard_map/ppermute | solution.py:565
  21.5 26.6 %copy-start.23 = (f32[48,256]{1,0:T(8,128)}, f32[48,256]{1,0:T(8,128)S(1)}, u32[]{:S(2)}) copy-start(f32[48,256]{1,0:T(8,128)S(1)} %select_maximum_fusion.refs_4_.refs_6_) | copy-start | bytes 147460
  36.1 27.2 %collective-permute-start.1 = (f32[128,1024]{1,0:T(8,128)S(1)}, f32[128,1024]{1,0:T(8,128)S(1)}, u32[]{:S(2)}, u32[]{:S(2)}) collective-permute-start(f32[128,1024]{1,0:T(8,128)S(1)} %collective-permute-done), channel_id=1, source_target_pairs={{0,8},{4,12},{8,0},{12,4},{16,24},{20,28},{24,16},{28,20},{1,9},{5... | collective-permute-start | bytes 1572872 | tf_op jit(solution)/shard_map/ppermute | solution.py:568
  37.7 25.6 %collective-permute-start.2 = (f32[128,1024]{1,0:T(8,128)S(1)}, f32[128,1024]{1,0:T(8,128)S(1)}, u32[]{:S(2)}, u32[]{:S(2)}) collective-permute-start(f32[128,1024]{1,0:T(8,128)S(1)} %collective-permute-done), channel_id=1, source_target_pairs={{0,16},{4,20},{8,24},{12,28},{16,0},{20,4},{24,8},{28,12},{1,17},{... | collective-permute-start | bytes 1572872 | tf_op jit(solution)/shard_map/ppermute | solution.py:568
  39.2 6.2 %collective-permute-start.4 = (f32[48,256]{1,0:T(8,128)S(1)}, f32[48,256]{1,0:T(8,128)S(1)}, u32[]{:S(2)}, u32[]{:S(2)}) collective-permute-start(f32[48,256]{1,0:T(8,128)S(1)} %select_maximum_fusion.refs_4_.refs_6_), channel_id=1, source_target_pairs={{0,1},{1,0},{2,3},{3,2},{4,5},{5,4},{6,7},{7,6},{8,9},{9,8},{10,11... | collective-permute-start | bytes 147464 | tf_op jit(solution)/shard_map/ppermute | solution.py:565
  39.2 24.0 %collective-permute-start.5 = (f32[48,256]{1,0:T(8,128)S(1)}, f32[48,256]{1,0:T(8,128)S(1)}, u32[]{:S(2)}, u32[]{:S(2)}) collective-permute-start(f32[48,256]{1,0:T(8,128)S(1)} %select_maximum_fusion.refs_4_.refs_6_), channel_id=1, source_target_pairs={{0,2},{1,3},{2,0},{3,1},{4,6},{5,7},{6,4},{7,5},{8,10},{9,11},{10,... | collective-permute-start | bytes 147464 | tf_op jit(solution)/shard_map/ppermute | solution.py:565
  45.4 17.8 %collective-permute-start.6 = (f32[48,256]{1,0:T(8,128)S(1)}, f32[48,256]{1,0:T(8,128)S(1)}, u32[]{:S(2)}, u32[]{:S(2)}) collective-permute-start(f32[48,256]{1,0:T(8,128)S(1)} %select_maximum_fusion.refs_4_.refs_6_), channel_id=1, source_target_pairs={{0,3},{1,2},{2,1},{3,0},{4,7},{5,6},{6,5},{7,4},{8,11},{9,10},{10,... | collective-permute-start | bytes 147464 | tf_op jit(solution)/shard_map/ppermute | solution.py:565
  63.3 13.4 %collective-permute-start.10 = (f32[128,1024]{1,0:T(8,128)S(1)}, f32[128,1024]{1,0:T(8,128)S(1)}, u32[]{:S(2)}, u32[]{:S(2)}) collective-permute-start(f32[128,1024]{1,0:T(8,128)S(1)} %get-tuple-element.367), channel_id=1, source_target_pairs={{0,1},{1,0},{2,3},{3,2},{4,5},{5,4},{6,7},{7,6},{8,9},{9,8},{10,11... | collective-permute-start | bytes 1572872 | tf_op jit(solution)/shard_map/ppermute | solution.py:565
  77.0 4.2 collective-permute-start.11
  77.0 21.8 %collective-permute-start.9 = (f32[128,1024]{1,0:T(8,128)S(1)}, f32[128,1024]{1,0:T(8,128)S(1)}, u32[]{:S(2)}, u32[]{:S(2)}) collective-permute-start(f32[128,1024]{1,0:T(8,128)S(1)} %get-tuple-element.365), channel_id=1, source_target_pairs={{0,3},{1,2},{2,1},{3,0},{4,7},{5,6},{6,5},{7,4},{8,11},{9,10},{10,... | collective-permute-start | bytes 1572872 | tf_op jit(solution)/shard_map/ppermute | solution.py:565
  77.4 21.5 %collective-permute-start.7 = (f32[128,1024]{1,0:T(8,128)S(1)}, f32[128,1024]{1,0:T(8,128)S(1)}, u32[]{:S(2)}, u32[]{:S(2)}) collective-permute-start(f32[128,1024]{1,0:T(8,128)S(1)} %collective-permute-done.3), channel_id=1, source_target_pairs={{0,8},{4,12},{8,0},{12,4},{16,24},{20,28},{24,16},{28,20},{1,9},{5... | collective-permute-start | bytes 1572872 | tf_op jit(solution)/shard_map/ppermute | solution.py:568
  77.4 21.5 %collective-permute-start.8 = (f32[128,1024]{1,0:T(8,128)S(1)}, f32[128,1024]{1,0:T(8,128)S(1)}, u32[]{:S(2)}, u32[]{:S(2)}) collective-permute-start(f32[128,1024]{1,0:T(8,128)S(1)} %collective-permute-done.3), channel_id=1, source_target_pairs={{0,16},{4,20},{8,24},{12,28},{16,0},{20,4},{24,8},{28,12},{1,17},{... | collective-permute-start | bytes 1572872 | tf_op jit(solution)/shard_map/ppermute | solution.py:568
  98.9 19.9 %copy-start.21 = (f32[128,1024]{1,0:T(8,128)}, f32[128,1024]{1,0:T(8,128)S(1)}, u32[]{:S(2)}) copy-start(f32[128,1024]{1,0:T(8,128)S(1)} %collective-permute-done.9) | copy-start | bytes 1572868
  98.9 14.0 %collective-permute-start.15 = (f32[128,1024]{1,0:T(8,128)S(1)}, f32[128,1024]{1,0:T(8,128)S(1)}, u32[]{:S(2)}, u32[]{:S(2)}) collective-permute-start(f32[128,1024]{1,0:T(8,128)S(1)} %collective-permute-done.7), channel_id=1, source_target_pairs={{0,16},{4,20},{8,24},{12,28},{16,0},{20,4},{24,8},{28,12},{1,17},{... | collective-permute-start | bytes 1572872 | tf_op jit(solution)/shard_map/ppermute | solution.py:568
  113.1 6.0 %collective-permute-start.16 = (f32[512,1024]{1,0:T(8,128)S(1)}, f32[512,1024]{1,0:T(8,128)S(1)}, u32[]{:S(2)}, u32[]{:S(2)}) collective-permute-start(f32[512,1024]{1,0:T(8,128)S(1)} %constant_dynamic-update-slice_fusion.4.refs_1_), channel_id=1, source_target_pairs={{0,4},{4,0},{8,12},{12,8},{16,20},{20,16},{24,28},{28,24},{1,5},{5... | collective-permute-start | bytes 6291464 | tf_op jit(solution)/shard_map/ppermute | solution.py:568
  115.2 27.1 %collective-permute-start.14 = (f32[256,1024]{1,0:T(8,128)}, f32[256,1024]{1,0:T(8,128)}, u32[]{:S(2)}, u32[]{:S(2)}) collective-permute-start(f32[256,1024]{1,0:T(8,128)} %get-tuple-element.442), channel_id=1, source_target_pairs={{0,1},{1,0},{2,3},{3,2},{4,5},{5,4},{6,7},{7,6},{8,9},{9,8},{10,11... | collective-permute-start | bytes 3145736 | tf_op jit(solution)/shard_map/ppermute | solution.py:565
  118.8 18.0 %collective-permute-start.12 = (f32[128,1024]{1,0:T(8,128)S(1)}, f32[128,1024]{1,0:T(8,128)S(1)}, u32[]{:S(2)}, u32[]{:S(2)}) collective-permute-start(f32[128,1024]{1,0:T(8,128)S(1)} %collective-permute-done.9), channel_id=1, source_target_pairs={{0,8},{4,12},{8,0},{12,4},{16,24},{20,28},{24,16},{28,20},{1,9},{5... | collective-permute-start | bytes 1572872 | tf_op jit(solution)/shard_map/ppermute | solution.py:568
  118.8 18.0 %collective-permute-start.13 = (f32[128,1024]{1,0:T(8,128)S(1)}, f32[128,1024]{1,0:T(8,128)S(1)}, u32[]{:S(2)}, u32[]{:S(2)}) collective-permute-start(f32[128,1024]{1,0:T(8,128)S(1)} %collective-permute-done.9), channel_id=1, source_target_pairs={{0,16},{4,20},{8,24},{12,28},{16,0},{20,4},{24,8},{28,12},{1,17},{... | collective-permute-start | bytes 1572872 | tf_op jit(solution)/shard_map/ppermute | solution.py:568
  119.1 36.6 %copy-start.22 = (f32[128,1024]{1,0:T(8,128)S(1)}, f32[128,1024]{1,0:T(8,128)}, u32[]{:S(2)}) copy-start(f32[128,1024]{1,0:T(8,128)} %copy-done.21) | copy-start | bytes 1572868
  142.4 13.2 %collective-permute-start.17 = (f32[128,1024]{1,0:T(8,128)S(1)}, f32[128,1024]{1,0:T(8,128)S(1)}, u32[]{:S(2)}, u32[]{:S(2)}) collective-permute-start(f32[128,1024]{1,0:T(8,128)S(1)} %collective-permute-done.13), channel_id=1, source_target_pairs={{0,8},{4,12},{8,0},{12,4},{16,24},{20,28},{24,16},{28,20},{1,9},{5... | collective-permute-start | bytes 1572872 | tf_op jit(solution)/shard_map/ppermute | solution.py:568
  155.8 4.2 collective-permute-start.18
  155.9 49.4 %collective-permute-start.21 = (f32[256,1024]{1,0:T(8,128)}, f32[256,1024]{1,0:T(8,128)}, u32[]{:S(2)}, u32[]{:S(2)}) collective-permute-start(f32[256,1024]{1,0:T(8,128)} %get-tuple-element.442), channel_id=1, source_target_pairs={{0,2},{1,3},{2,0},{3,1},{4,6},{5,7},{6,4},{7,5},{8,10},{9,11},{10,... | collective-permute-start | bytes 3145736 | tf_op jit(solution)/shard_map/ppermute | solution.py:565
  157.3 48.0 %collective-permute-start.19 = (f32[256,1024]{1,0:T(8,128)}, f32[256,1024]{1,0:T(8,128)}, u32[]{:S(2)}, u32[]{:S(2)}) collective-permute-start(f32[256,1024]{1,0:T(8,128)} %collective-permute-done.14), channel_id=1, source_target_pairs={{0,8},{4,12},{8,0},{12,4},{16,24},{20,28},{24,16},{28,20},{1,9},{5... | collective-permute-start | bytes 3145736 | tf_op jit(solution)/shard_map/ppermute | solution.py:568
  157.6 47.7 %collective-permute-start.20 = (f32[256,1024]{1,0:T(8,128)}, f32[256,1024]{1,0:T(8,128)}, u32[]{:S(2)}, u32[]{:S(2)}) collective-permute-start(f32[256,1024]{1,0:T(8,128)} %collective-permute-done.14), channel_id=1, source_target_pairs={{0,16},{4,20},{8,24},{12,28},{16,0},{20,4},{24,8},{28,12},{1,17},{... | collective-permute-start | bytes 3145736 | tf_op jit(solution)/shard_map/ppermute | solution.py:568
  161.4 47.0 %collective-permute-start.25 = (f32[256,1024]{1,0:T(8,128)}, f32[256,1024]{1,0:T(8,128)}, u32[]{:S(2)}, u32[]{:S(2)}) collective-permute-start(f32[256,1024]{1,0:T(8,128)} %get-tuple-element.444), channel_id=1, source_target_pairs={{0,1},{1,0},{2,3},{3,2},{4,5},{5,4},{6,7},{7,6},{8,9},{9,8},{10,11... | collective-permute-start | bytes 3145736 | tf_op jit(solution)/shard_map/ppermute | solution.py:565
  217.8 14.8 %collective-permute-start.26 = (f32[1024,1024]{1,0:T(8,128)}, f32[1024,1024]{1,0:T(8,128)}, u32[]{:S(2)}, u32[]{:S(2)}) collective-permute-start(f32[1024,1024]{1,0:T(8,128)} %constant_dynamic-update-slice_fusion.12.mine_ref), channel_id=1, source_target_pairs={{0,4},{4,0},{8,12},{12,8},{16,20},{20,16},{24,28},{28,24},{1,5},{5... | collective-permute-start | bytes 12582920 | tf_op jit(solution)/shard_map/ppermute | solution.py:568
  217.8 28.7 %collective-permute-start.24 = (f32[256,1024]{1,0:T(8,128)}, f32[256,1024]{1,0:T(8,128)}, u32[]{:S(2)}, u32[]{:S(2)}) collective-permute-start(f32[256,1024]{1,0:T(8,128)} %get-tuple-element.442), channel_id=1, source_target_pairs={{0,3},{1,2},{2,1},{3,0},{4,7},{5,6},{6,5},{7,4},{8,11},{9,10},{10,... | collective-permute-start | bytes 3145736 | tf_op jit(solution)/shard_map/ppermute | solution.py:565
  219.1 27.4 %collective-permute-start.22 = (f32[256,1024]{1,0:T(8,128)}, f32[256,1024]{1,0:T(8,128)S(1)}, u32[]{:S(2)}, u32[]{:S(2)}) collective-permute-start(f32[256,1024]{1,0:T(8,128)} %collective-permute-done.21), channel_id=1, source_target_pairs={{0,8},{4,12},{8,0},{12,4},{16,24},{20,28},{24,16},{28,20},{1,9},{5... | collective-permute-start | bytes 3145736 | tf_op jit(solution)/shard_map/ppermute | solution.py:568
  219.4 27.1 %collective-permute-start.23 = (f32[256,1024]{1,0:T(8,128)}, f32[256,1024]{1,0:T(8,128)S(1)}, u32[]{:S(2)}, u32[]{:S(2)}) collective-permute-start(f32[256,1024]{1,0:T(8,128)} %collective-permute-done.21), channel_id=1, source_target_pairs={{0,16},{4,20},{8,24},{12,28},{16,0},{20,4},{24,8},{28,12},{1,17},{... | collective-permute-start | bytes 3145736 | tf_op jit(solution)/shard_map/ppermute | solution.py:568
  246.5 24.8 %collective-permute-start.29 = (f32[256,1024]{1,0:T(8,128)S(1)}, f32[256,1024]{1,0:T(8,128)S(1)}, u32[]{:S(2)}, u32[]{:S(2)}) collective-permute-start(f32[256,1024]{1,0:T(8,128)S(1)} %collective-permute-done.22), channel_id=1, source_target_pairs={{0,16},{4,20},{8,24},{12,28},{16,0},{20,4},{24,8},{28,12},{1,17},{... | collective-permute-start | bytes 3145736 | tf_op jit(solution)/shard_map/ppermute | solution.py:568
  273.4 7.2 %collective-permute-start.30 = (f32[1024,1024]{1,0:T(8,128)S(1)}, f32[1024,1024]{1,0:T(8,128)S(1)}, u32[]{:S(2)}, u32[]{:S(2)}) collective-permute-start(f32[1024,1024]{1,0:T(8,128)S(1)} %constant_dynamic-update-slice_fusion.16.mine_ref), channel_id=1, source_target_pairs={{0,4},{4,0},{8,12},{12,8},{16,20},{20,16},{24,28},{28,24},{1,5},{5... | collective-permute-start | bytes 12582920 | tf_op jit(solution)/shard_map/ppermute | solution.py:568
  273.5 25.8 %collective-permute-start.27 = (f32[256,1024]{1,0:T(8,128)}, f32[256,1024]{1,0:T(8,128)S(1)}, u32[]{:S(2)}, u32[]{:S(2)}) collective-permute-start(f32[256,1024]{1,0:T(8,128)} %collective-permute-done.24), channel_id=1, source_target_pairs={{0,8},{4,12},{8,0},{12,4},{16,24},{20,28},{24,16},{28,20},{1,9},{5... | collective-permute-start | bytes 3145736 | tf_op jit(solution)/shard_map/ppermute | solution.py:568
  274.0 25.5 %collective-permute-start.28 = (f32[256,1024]{1,0:T(8,128)}, f32[256,1024]{1,0:T(8,128)S(1)}, u32[]{:S(2)}, u32[]{:S(2)}) collective-permute-start(f32[256,1024]{1,0:T(8,128)} %collective-permute-done.24), channel_id=1, source_target_pairs={{0,16},{4,20},{8,24},{12,28},{16,0},{20,4},{24,8},{28,12},{1,17},{... | collective-permute-start | bytes 3145736 | tf_op jit(solution)/shard_map/ppermute | solution.py:568
  301.1 5.7 %collective-permute-start.33 = (f32[768,1024]{1,0:T(8,128)S(1)}, f32[768,1024]{1,0:T(8,128)S(1)}, u32[]{:S(2)}, u32[]{:S(2)}) collective-permute-start(f32[768,1024]{1,0:T(8,128)S(1)} %constant_dynamic-update-slice_fusion.20.mine_ref), channel_id=1, source_target_pairs={{0,4},{4,0},{8,12},{12,8},{16,20},{20,16},{24,28},{28,24},{1,5},{5... | collective-permute-start | bytes 9437192 | tf_op jit(solution)/shard_map/ppermute | solution.py:568
  301.2 19.3 %collective-permute-start.32 = (f32[128,1024]{1,0:T(8,128)S(1)}, f32[128,1024]{1,0:T(8,128)S(1)}, u32[]{:S(2)}, u32[]{:S(2)}) collective-permute-start(f32[128,1024]{1,0:T(8,128)S(1)} %slice.89), channel_id=1, source_target_pairs={{0,8},{4,12},{8,0},{12,4},{16,24},{20,28},{24,16},{28,20},{1,9},{5... | collective-permute-start | bytes 1572872 | tf_op jit(solution)/shard_map/ppermute | solution.py:568
  302.9 17.6 %collective-permute-start.31 = (f32[128,1024]{1,0:T(8,128)S(1)}, f32[128,1024]{1,0:T(8,128)S(1)}, u32[]{:S(2)}, u32[]{:S(2)}) collective-permute-start(f32[128,1024]{1,0:T(8,128)S(1)} %slice.88), channel_id=1, source_target_pairs={{0,16},{4,20},{8,24},{12,28},{16,0},{20,4},{24,8},{28,12},{1,17},{... | collective-permute-start | bytes 1572872 | tf_op jit(solution)/shard_map/ppermute | solution.py:568
  320.6 2.7 collective-permute-start.34
  368.5 144.1 %reduce-scatter.5.cloned.1.call-start = ((), (), s32[]{:S(2)}) async-start(), calls=%async_computation.3 | async-start | bytes 9437184 | tf_op jit(solution)/shard_map/reduce_scatter | solution.py:690
  371.9 18.2 %collective-permute-start.35 = (f32[64,256]{1,0:T(8,128)S(1)}, f32[64,256]{1,0:T(8,128)S(1)}, u32[]{:S(2)}, u32[]{:S(2)}) collective-permute-start(f32[64,256]{1,0:T(8,128)S(1)} %concatenate.35), channel_id=1, source_target_pairs={{0,4},{4,0},{8,12},{12,8},{16,20},{20,16},{24,28},{28,24},{1,5},{5... | collective-permute-start | bytes 196616 | tf_op jit(solution)/shard_map/ppermute | solution.py:568
  390.2 20.9 %collective-permute-start.36 = (f32[64,256]{1,0:T(8,128)S(1)}, f32[64,256]{1,0:T(8,128)S(1)}, u32[]{:S(2)}, u32[]{:S(2)}) collective-permute-start(f32[64,256]{1,0:T(8,128)S(1)} %add.70), channel_id=1, source_target_pairs={{0,8},{4,12},{8,0},{12,4},{16,24},{20,28},{24,16},{28,20},{1,9},{5... | collective-permute-start | bytes 196616 | tf_op jit(solution)/shard_map/ppermute | solution.py:568
  411.1 18.8 %collective-permute-start.37 = (f32[64,256]{1,0:T(8,128)S(1)}, f32[64,256]{1,0:T(8,128)S(1)}, u32[]{:S(2)}, u32[]{:S(2)}) collective-permute-start(f32[64,256]{1,0:T(8,128)S(1)} %add.71), channel_id=1, source_target_pairs={{0,16},{4,20},{8,24},{12,28},{16,0},{20,4},{24,8},{28,12},{1,17},{... | collective-permute-start | bytes 196616 | tf_op jit(solution)/shard_map/ppermute | solution.py:568
  429.9 28.8 %collective-permute-start.38 = (f32[64,256]{1,0:T(8,128)S(1)}, f32[64,256]{1,0:T(8,128)S(1)}, u32[]{:S(2)}, u32[]{:S(2)}) collective-permute-start(f32[64,256]{1,0:T(8,128)S(1)} %add.72), channel_id=1, source_target_pairs={{0,1},{1,0},{2,3},{3,2},{4,5},{5,4},{6,7},{7,6},{8,9},{9,8},{10,11... | collective-permute-start | bytes 196616 | tf_op jit(solution)/shard_map/ppermute | solution.py:565
  458.7 5.8 %collective-permute-start.39 = (f32[64,256]{1,0:T(8,128)S(1)}, f32[64,256]{1,0:T(8,128)S(1)}, u32[]{:S(2)}, u32[]{:S(2)}) collective-permute-start(f32[64,256]{1,0:T(8,128)S(1)} %add.73), channel_id=1, source_target_pairs={{0,2},{1,3},{2,0},{3,1},{4,6},{5,7},{6,4},{7,5},{8,10},{9,11},{10,... | collective-permute-start | bytes 196616 | tf_op jit(solution)/shard_map/ppermute | solution.py:565
  464.6 1.9 collective-permute-start.40
  466.5 3.8 collective-permute-start.41
  470.3 4.0 collective-permute-start.42
  (33 other events, 189.2 us)
Sparse Core Ops, SparseCore 0:
  368.6 68.5 reduce-scatter.2
  441.1 71.5 reduce-scatter.4
